TPU v7x, 512 devices: a whole 4x4x16 slice. The times are simulated.
512 devices in a mesh: win: 32 (over y, z_hi, x), tile: 16 (over z_lo, core).
Axes of the slice: x: 4, y: 4, z: 16 (z_hi: 2, z_lo: 8; z = z_hi * 8 + z_lo), core: 2. Of those that a mesh axis runs over, the one named last changes fastest.
Arguments:
- latents: bfloat16 [32, 16, 16, 2, 20, 320], P('win', None, 'tile'), may hold values from -40 to 40
- spatial_weight: bfloat16 [3, 3, 320, 320], replicated, may hold values from -0.109375 to 0.109375
- temporal_weight: bfloat16 [3, 320, 320], replicated, may hold values from -0.1875 to 0.1875
- gain_first: float32 [320], replicated, may hold values from 0.5 to 1.5
- shift_first: float32 [320], replicated, may hold values from -0.5 to 0.5
- gain_second: float32 [320], replicated, may hold values from 0.5 to 1.5
- shift_second: float32 [320], replicated, may hold values from -0.5 to 0.5
- temporal_bias: float32 [320], replicated, may hold values from -0.5 to 0.5
- starts: int32 [32], replicated, may hold values from 0 to 310, as said below
- blend_counts: int32 [32, 16], replicated, may hold values from 1 to 8
Outputs:
- joined: bfloat16 [32, 16, 16, 2, 20, 320], P('win', None, 'tile')
Inputs may be any that keep to these rules, and one draw needn't show every extreme that they name: starts[0] is 0; consecutive starts rise by 8 to 12, by exactly 8 for at least one pair and by exactly 12 for at least one other pair; the last start is 310.
All inputs are finite; a program needn't handle non-finite values.
Results may differ from a plain program's by a relative error of at most 0.007.
Values may be sent and summed in bfloat16 or wider, within the bound.
A program may use at most 64 MiB of HBM per device.

v0:
```python
import jax
import jax.numpy as jnp
from jax import lax
from jax.sharding import PartitionSpec as P

NORM_GROUPS = 32
SHARED_FRAMES = 8
TCOLS = 4


EPSILON = 1e-05


def passed_along(array, axis, by):
    length = lax.axis_size(axis)
    pairs = [(i, i + by) for i in range(length) if 0 <= i + by < length]
    return lax.ppermute(array, axis, pairs)


def group_sums(field):
    grouped = field.reshape(-1, NORM_GROUPS, field.shape[-1] // NORM_GROUPS)
    return (jnp.sum(grouped, axis=(0, 2)), jnp.sum(grouped * grouped, axis=(0, 2)))


def normalize(field, totals, members, gain, shift):
    channels = field.shape[-1]
    group_mean = totals[0] / members
    spread = totals[1] / members - group_mean * group_mean
    inverse = lax.rsqrt(spread + EPSILON)
    return (field - jnp.repeat(group_mean, channels // NORM_GROUPS)) * jnp.repeat(
        inverse, channels // NORM_GROUPS
    ) * gain + shift


def first_totals(floated):
    return lax.psum(group_sums(floated), "tile")


def rows_from(piece, steps):
    return passed_along(piece, "tile", steps)


def cols_from(piece, steps):
    return passed_along(piece, "tile", steps)


def extend(latent_grid, column):
    height = latent_grid.shape[1]
    taller = jnp.concatenate(
        [
            rows_from(latent_grid[:, height - 1 :], TCOLS),
            latent_grid,
            rows_from(latent_grid[:, :1], -TCOLS),
        ],
        axis=1,
    )
    across = taller.shape[2]
    left_rim = cols_from(taller[:, :, across - 1 :], 1)
    right_rim = cols_from(taller[:, :, :1], -1)
    left_rim = jnp.where(column > 0, left_rim, jnp.zeros_like(left_rim))
    right_rim = jnp.where(column < TCOLS - 1, right_rim, jnp.zeros_like(right_rim))
    return jnp.concatenate([left_rim, taller, right_rim], axis=2)


def spatial_conv(activated, weight):
    frames, rows_ext, cols_ext, channels = activated.shape
    height = rows_ext - 2
    across = cols_ext - 2
    summed = jnp.zeros((frames * height * across, weight.shape[3]), jnp.float32)
    for offset_row in range(3):
        for offset_col in range(3):
            piece = activated[
                :, offset_row : offset_row + height, offset_col : offset_col + across
            ].reshape(-1, channels)
            summed = summed + jnp.dot(
                piece, weight[offset_row, offset_col], preferred_element_type=jnp.float32
            )
    return summed.reshape(frames, height, across, -1)


def on_device(
    latents,
    spatial_weight,
    temporal_weight,
    gain_first,
    shift_first,
    gain_second,
    shift_second,
    temporal_bias,
    starts,
    blend_counts,
):
    frames = latents.shape[1]
    height = latents.shape[3]
    across = latents.shape[4]
    channels = latents.shape[5]
    latent_grid = latents.reshape(frames, height, across, channels)
    tile_count = lax.axis_size("tile")
    position = lax.axis_index("tile")
    column = position % TCOLS
    members = frames * height * across * tile_count * (channels // NORM_GROUPS)
    floated = latent_grid.astype(jnp.float32)
    totals = first_totals(floated)
    activated = extend(
        jax.nn.silu(normalize(floated, totals, members, gain_first, shift_first)).astype(
            jnp.bfloat16
        ),
        column,
    )
    spatial = spatial_conv(activated, spatial_weight).astype(jnp.bfloat16)
    spatial_single_float = spatial.astype(jnp.float32)
    second = lax.psum(group_sums(spatial_single_float), "tile")
    mixed = jax.nn.silu(
        normalize(spatial_single_float, second, members, gain_second, shift_second)
    ).astype(jnp.bfloat16)
    flat = mixed.reshape(frames, height * across, channels)
    empty = jnp.zeros((1, height * across, channels), jnp.bfloat16)
    framed = jnp.concatenate([empty, flat, empty], axis=0)
    running = floated.reshape(-1, channels) + temporal_bias
    for tap in range(3):
        running = running + jnp.dot(
            framed[tap : tap + frames].reshape(-1, channels),
            temporal_weight[tap],
            preferred_element_type=jnp.float32,
        )
    block = running.astype(jnp.bfloat16).reshape(frames, -1)
    windows = lax.axis_size("win")
    window_index = lax.axis_index("win")
    slots = jnp.arange(windows)

    def pick(offset):
        matched = slots == window_index + offset
        return (
            jnp.sum(jnp.where(matched, starts, 0)),
            jnp.sum(jnp.where(matched[:, None], blend_counts, 0), axis=0),
        )

    start_own, counts_own = pick(0)
    start_prev, previous_counts = pick(-1)
    start_next, counts_next = pick(1)
    gap_prev = start_own - start_prev
    gap_next = start_next - start_own
    frame_ids = jnp.arange(frames)[:, None]
    slot_ids = jnp.arange(SHARED_FRAMES)[None, :]
    prev_weights = jnp.where(
        slot_ids == frame_ids + gap_prev - (frames - SHARED_FRAMES),
        previous_counts[frames - SHARED_FRAMES :][None, :],
        0,
    ).astype(jnp.float32)
    next_weights = jnp.where(
        slot_ids == frame_ids - gap_next, counts_next[:SHARED_FRAMES][None, :], 0
    ).astype(jnp.float32)
    own_weights = counts_own.astype(jnp.float32)
    prev_tail = passed_along(block[frames - SHARED_FRAMES :], "win", 1)
    next_head = passed_along(block[:SHARED_FRAMES], "win", -1)
    numer = own_weights[:, None] * block.astype(jnp.float32)
    numer = numer + jnp.dot(
        prev_weights.astype(jnp.bfloat16), prev_tail, preferred_element_type=jnp.float32
    )
    numer = numer + jnp.dot(
        next_weights.astype(jnp.bfloat16), next_head, preferred_element_type=jnp.float32
    )
    denom = own_weights + jnp.sum(prev_weights, axis=1) + jnp.sum(next_weights, axis=1)
    joined = (numer / denom[:, None]).astype(jnp.bfloat16)
    return joined.reshape(1, frames, 1, height, across, channels)


def solution(mesh):
    return jax.shard_map(
        on_device,
        mesh=mesh,
        in_specs=(
            P("win", None, "tile", None, None, None),
            P(),
            P(),
            P(),
            P(),
            P(),
            P(),
            P(),
            P(),
            P(),
        ),
        out_specs=P("win", None, "tile", None, None, None),
        check_vma=False,
    )
```

profile of v0, /device:TPU:24, one launch (start us, length us, event | category | flops | bytes accessed | tf_op | source)
XLA Modules:
  0.0 202.8 jit_solution(11549313151482653165)
XLA Ops:
  0.0 2.0 convert_reduce_fusion
  2.4 56.2 %all-reduce.3 = (f32[32]{0:T(128)S(1)}, f32[32]{0:T(128)S(1)}) all-reduce(f32[32]{0:T(128)S(1)} %reduce_sum.142, f32[32]{0:T(128)S(1)} %reduce_sum.139), channel_id=1, replica_groups=mesh['win'=32,'tile'=16] {'tile'}, use_global_device_ids=true, to_apply=%region_6.7 | all-reduce | flops 64 | bytes 512 | tf_op jit(solution)/shard_map/psum | solution.py:36
  59.0 2.5 %fusion.14 = bf16[16,2,20,320]{3,1,2,0:T(2,128)(2,1)S(1)} fusion(bf16[1,16,1,2,20,320]{5,3,4,2,1,0:T(2,128)(2,1)} %param.10, f32[320]{0:T(512)} %param.14, f32[320]{0:T(512)} %param.13, f32[320]{0:T(512)S(1)} %mul.100, f32[320]{0:T(512)S(1)} %sub.58), kind=kLoop, calls=%fused_computation.35 | loop fusion | flops 2048000 | bytes 824320 | tf_op jit(solution)/shard_map/convert_element_type | solution.py:105
  61.5 1.6 fusion.58
  63.1 1.3 collective-permute-start
  64.5 1.3 collective-permute-start.1
  65.8 2.2 %fusion.13 = bf16[1,16,1,2,20,320]{5,3,4,2,1,0:T(2,128)(2,1)} fusion(bf16[1,16,1,2,20,320]{5,3,4,2,1,0:T(2,128)(2,1)S(1)} %copy-done, f32[320]{0:T(512)S(1)} %copy-done.8, f32[320]{0:T(512)S(1)} %copy-done.9, f32[320]{0:T(512)S(1)} %mul.100, f32[320]{0:T(512)S(1)} %sub.58), kind=kLoop, calls=%fused_computation.34 | loop fusion | flops 2048000 | bytes 824320 | tf_op jit(solution)/shard_map/convert_element_type | solution.py:105
  71.7 1.1 copy.35
  74.8 1.5 copy.30
  76.5 3.1 %collective-permute-done.1 = bf16[16,1,20,320]{3,1,2,0:T(2,128)(2,1)S(1)} collective-permute-done((bf16[16,1,20,320]{3,1,2,0:T(2,128)(2,1)}, bf16[16,1,20,320]{3,1,2,0:T(2,128)(2,1)S(1)}, u32[]{:S(2)}, u32[]{:S(2)}) %collective-permute-start.1) | collective-permute-done | bytes 204832 | tf_op jit(solution)/shard_map/ppermute | solution.py:17
  79.8 1.3 collective-permute-start.3
  81.1 3.2 %collective-permute-start.2 = (bf16[16,4,1,320]{3,1,2,0:T(4,128)(2,1)S(1)}, bf16[16,4,1,320]{3,1,2,0:T(4,128)(2,1)S(1)}, u32[]{:S(2)}, u32[]{:S(2)}) collective-permute-start(bf16[16,4,1,320]{3,1,2,0:T(4,128)(2,1)S(1)} %get-tuple-element.22), channel_id=1, source_target_pairs={{0,1},{1,2},{2,3},{3,4},{4,5},{5,6},{6,7},{7,8},{8,9},{9,10},{10,1... | collective-permute-start | bytes 122888 | tf_op jit(solution)/shard_map/ppermute | solution.py:17
  84.3 2.3 %pad_maximum_fusion.1 = (bf16[16,2,20,320]{3,1,2,0:T(2,128)(2,1)S(1)}, bf16[16,2,20,320]{3,1,2,0:T(2,128)(2,1)S(1)}) fusion(bf16[16,1,20,320]{3,1,2,0:T(2,128)(2,1)S(1)} %collective-permute-done.1, bf16[16,2,20,320]{3,1,2,0:T(2,128)(2,1)S(1)} %fusion.14, bf16[16,1,20,320]{3,1,2,0:T(2,128)(2,1)S(1)} %collective-permute-done), kind=kLoop, calls=%fused_computation.40 | loop fusion | flops 1638400 | bytes 1638400 | tf_op jit(solution)/shard_map/concatenate | solution.py:49
  88.9 3.6 %pad_maximum_fusion = (bf16[16,4,21,320]{3,1,2,0:T(4,128)(2,1)S(1)}, bf16[16,4,21,320]{3,1,2,0:T(4,128)(2,1)S(1)}) fusion(bf16[16,4,1,320]{3,1,2,0:T(4,128)(2,1)S(1)} %broadcast_select_fusion, bf16[16,1,20,320]{3,1,2,0:T(2,128)(2,1)S(1)} %collective-permute-done.1, bf16[16,2,20,320]{3,1,2,0:T(2,128)(2,1)S(1)} %fusion.14, ...), kind=kLoop, calls=%fused_computation.19 | loop fusion | flops 6881280 | bytes 2621440 | tf_op jit(solution)/shard_map/concatenate | solution.py:62
  92.6 3.2 %fusion.56 = (bf16[16,2,20,320]{3,1,2,0:T(2,128)(2,1)S(1)}, bf16[16,2,20,320]{3,1,2,0:T(2,128)(2,1)S(1)}, bf16[16,2,20,320]{3,1,2,0:T(2,128)(2,1)}, bf16[16,2,20...) fusion(bf16[16,4,21,320]{3,1,2,0:T(4,128)(2,1)S(1)} %get-tuple-element.19, ...), kind=kLoop, calls=%fused_computation.110 | loop fusion | bytes 4915200 | tf_op jit(solution)/shard_map/slice | solution.py:72
  96.3 1.1 copy.33
  98.5 1.1 copy.31
  104.8 1.7 fusion.31
  106.5 1.5 convolution_add_fusion.11
  112.1 47.6 %all-reduce.2 = (f32[32]{0:T(128)S(1)}, f32[32]{0:T(128)S(1)}) all-reduce(f32[32]{0:T(128)S(1)} %reduce_sum.148, f32[32]{0:T(128)S(1)} %reduce_sum.145), channel_id=1, replica_groups=mesh['win'=32,'tile'=16] {'tile'}, use_global_device_ids=true, to_apply=%region_12.13 | all-reduce | flops 64 | bytes 512 | tf_op jit(solution)/shard_map/psum | solution.py:112
  163.4 16.9 %collective-permute-start.5 = (bf16[8,12800]{1,0:T(8,128)(2,1)S(1)}, bf16[8,12800]{1,0:T(8,128)(2,1)S(1)}, u32[]{:S(2)}, u32[]{:S(2)}) collective-permute-start(bf16[8,12800]{1,0:T(8,128)(2,1)S(1)} %slice.137), channel_id=1, source_target_pairs={{16,0},{32,16},{48,32},{64,48},{80,64},{96,80},{112,96},{128,112},... | collective-permute-start | bytes 614408 | tf_op jit(solution)/shard_map/ppermute | solution.py:17
  180.9 1.9 collective-permute-start.4
  184.6 16.1 %collective-permute-done.4 = bf16[8,12800]{1,0:T(8,128)(2,1)S(1)} collective-permute-done((bf16[8,12800]{1,0:T(8,128)(2,1)S(1)}, bf16[8,12800]{1,0:T(8,128)(2,1)S(1)}, u32[]{:S(2)}, u32[]{:S(2)}) %collective-permute-start.4) | collective-permute-done | bytes 204832 | tf_op jit(solution)/shard_map/ppermute | solution.py:17
  201.7 1.2 copy.44
  (106 shorter events, 24.2 us)
Async XLA Ops:
  0.0 65.8 %copy-start = (bf16[1,16,1,2,20,320]{5,3,4,2,1,0:T(2,128)(2,1)S(1)}, bf16[1,16,1,2,20,320]{5,3,4,2,1,0:T(2,128)(2,1)}, u32[]{:S(2)}) copy-start(bf16[1,16,1,2,20,320]{5,3,4,2,1,0:T(2,128)(2,1)} %param.10) | copy-start | bytes 1228804
  0.0 65.8 %copy-start.8 = (f32[320]{0:T(512)S(1)}, f32[320]{0:T(512)}, u32[]{:S(2)}) copy-start(f32[320]{0:T(512)} %param.14) | copy-start | bytes 3844
  0.0 65.8 %copy-start.9 = (f32[320]{0:T(512)S(1)}, f32[320]{0:T(512)}, u32[]{:S(2)}) copy-start(f32[320]{0:T(512)} %param.13) | copy-start | bytes 3844
  61.5 6.6 %copy-start.14 = (s32[32]{0:T(128)S(1)}, s32[32]{0:T(128)}, u32[]{:S(2)}) copy-start(s32[32]{0:T(128)} %param.18) | copy-start | bytes 388
  61.5 9.9 %copy-start.10 = (s32[32,16]{0,1:T(8,128)S(1)}, s32[32,16]{0,1:T(8,128)}, u32[]{:S(2)}) copy-start(s32[32,16]{0,1:T(8,128)} %param.19) | copy-start | bytes 6148
  63.1 13.4 %collective-permute-start = (bf16[16,1,20,320]{3,1,2,0:T(2,128)(2,1)}, bf16[16,1,20,320]{3,1,2,0:T(2,128)(2,1)S(1)}, u32[]{:S(2)}, u32[]{:S(2)}) collective-permute-start(bf16[16,1,20,320]{3,1,2,0:T(2,128)(2,1)} %get-tuple-element.33), channel_id=1, source_target_pairs={{0,4},{1,5},{2,6},{3,7},{4,8},{5,9},{6,10},{7,11},{8,12},{9,13},{1... | collective-permute-start | bytes 614408 | tf_op jit(solution)/shard_map/ppermute | solution.py:17
  64.5 15.2 %collective-permute-start.1 = (bf16[16,1,20,320]{3,1,2,0:T(2,128)(2,1)}, bf16[16,1,20,320]{3,1,2,0:T(2,128)(2,1)S(1)}, u32[]{:S(2)}, u32[]{:S(2)}) collective-permute-start(bf16[16,1,20,320]{3,1,2,0:T(2,128)(2,1)} %get-tuple-element.34), channel_id=1, source_target_pairs={{4,0},{5,1},{6,2},{7,3},{8,4},{9,5},{10,6},{11,7},{12,8},{13,9},{1... | collective-permute-start | bytes 614408 | tf_op jit(solution)/shard_map/ppermute | solution.py:17
  79.8 8.2 %collective-permute-start.3 = (bf16[16,4,1,320]{3,1,2,0:T(4,128)(2,1)S(1)}, bf16[16,4,1,320]{3,1,2,0:T(4,128)(2,1)}, u32[]{:S(2)}, u32[]{:S(2)}) collective-permute-start(bf16[16,4,1,320]{3,1,2,0:T(4,128)(2,1)S(1)} %get-tuple-element.21), channel_id=1, source_target_pairs={{1,0},{2,1},{3,2},{4,3},{5,4},{6,5},{7,6},{8,7},{9,8},{10,9},{11,1... | collective-permute-start | bytes 122888 | tf_op jit(solution)/shard_map/ppermute | solution.py:17
  81.1 7.8 %collective-permute-start.2 = (bf16[16,4,1,320]{3,1,2,0:T(4,128)(2,1)S(1)}, bf16[16,4,1,320]{3,1,2,0:T(4,128)(2,1)S(1)}, u32[]{:S(2)}, u32[]{:S(2)}) collective-permute-start(bf16[16,4,1,320]{3,1,2,0:T(4,128)(2,1)S(1)} %get-tuple-element.22), channel_id=1, source_target_pairs={{0,1},{1,2},{2,3},{3,4},{4,5},{5,6},{6,7},{7,8},{8,9},{9,10},{10,1... | collective-permute-start | bytes 122888 | tf_op jit(solution)/shard_map/ppermute | solution.py:17
  104.8 3.2 %copy-start.1 = (bf16[3,3,320,320]{3,2,1,0:T(8,128)(2,1)S(1)}, bf16[3,3,320,320]{3,2,1,0:T(8,128)(2,1)}, u32[]{:S(2)}) copy-start(bf16[3,3,320,320]{3,2,1,0:T(8,128)(2,1)} %param.11) | copy-start | bytes 5529604
  104.8 3.2 %copy-start.4 = (bf16[640,320]{1,0:T(8,128)(2,1)S(1)}, bf16[640,320]{1,0:T(8,128)(2,1)}, u32[]{:S(2)}) copy-start(bf16[640,320]{1,0:T(8,128)(2,1)} %reshape.128) | copy-start | bytes 1228804
  106.5 2.0 copy-start.6
  108.0 1.0 copy-start.2
  109.0 1.0 copy-start.5
  109.5 1.1 copy-start.3
  111.0 49.4 %copy-start.11 = (f32[320]{0:T(512)S(1)}, f32[320]{0:T(512)}, u32[]{:S(2)}) copy-start(f32[320]{0:T(512)} %param.16) | copy-start | bytes 3844
  111.1 49.4 %copy-start.12 = (f32[320]{0:T(512)S(1)}, f32[320]{0:T(512)}, u32[]{:S(2)}) copy-start(f32[320]{0:T(512)} %param.15) | copy-start | bytes 3844
  160.1 1.1 copy-start.7
  160.1 1.1 copy-start.13
  163.4 20.8 %collective-permute-start.5 = (bf16[8,12800]{1,0:T(8,128)(2,1)S(1)}, bf16[8,12800]{1,0:T(8,128)(2,1)S(1)}, u32[]{:S(2)}, u32[]{:S(2)}) collective-permute-start(bf16[8,12800]{1,0:T(8,128)(2,1)S(1)} %slice.137), channel_id=1, source_target_pairs={{16,0},{32,16},{48,32},{64,48},{80,64},{96,80},{112,96},{128,112},... | collective-permute-start | bytes 614408 | tf_op jit(solution)/shard_map/ppermute | solution.py:17
  180.9 19.7 %collective-permute-start.4 = (bf16[8,12800]{1,0:T(8,128)(2,1)S(1)}, bf16[8,12800]{1,0:T(8,128)(2,1)S(1)}, u32[]{:S(2)}, u32[]{:S(2)}) collective-permute-start(bf16[8,12800]{1,0:T(8,128)(2,1)S(1)} %slice.134), channel_id=1, source_target_pairs={{0,16},{16,32},{32,48},{48,64},{64,80},{80,96},{96,112},{112,128},... | collective-permute-start | bytes 614408 | tf_op jit(solution)/shard_map/ppermute | solution.py:17
where the time goes:
time: 204 us; the launch traced here: 203 us
  blocking collectives  104 us (51%)
  starting transfers between devices  25.9 us (13%)
  local copies, waits for them, and re-layouts  25.2 us (12%)
  waiting for transfers between devices  20.3 us (10%)
  other arithmetic  15.6 us (8%)
  matrix products  8.92 us (4%)
  between operations  3.12 us (2%)
    psum x1, blocking collectives, first_totals(): return lax.psum(group_sums(floated), 'tile')  56.2 us
    psum x1, blocking collectives, on_device(): second = lax.psum(group_sums(spatial_single_float), 'tile')  47.6 us
    ppermute x6, starting transfers between devices, passed_along(): return lax.ppermute(array, axis, pairs)  25.9 us
    ppermute x6, waiting for transfers between devices, passed_along(): return lax.ppermute(array, axis, pairs)  20.3 us
    slice x9, local copies, waits for them, and re-layouts, spatial_conv(): activated[:, offset_row:offset_row + height, offset_col:offset_col + across]  7.94 us
    dot_general x9, matrix products, spatial_conv(): jnp.dot(piece, weight[offset_row, offset_col], preferred_element_type=jnp...  6.53 us
    reshape x8, local copies, waits for them, and re-layouts, spatial_conv(): piece = activated[:, offset_row:offset_row + height, offset_col:offset_co...  5.58 us
    convert_element_type x2, other arithmetic, on_device(): jax.nn.silu(normalize(floated, totals, members, gain_first, shift_first))  4.63 us
  transfers between devices with their start and end apart: 6, of which 3 were waited for; matrix products, arithmetic and copies ran while one was open for 7% of the time, Pallas kernels for 0%

commit v1 on v0

v1 whole, which is shorter than its diff:
```python
import jax
import jax.numpy as jnp
from jax import lax
from jax.experimental import pallas as pl
from jax.experimental.pallas import tpu as pltpu
from jax.sharding import PartitionSpec as P

MESH = pl.DeviceIdType.MESH
F32 = jnp.float32
BF16 = jnp.bfloat16

GROUPS = 32
EPSILON = 1e-05
FRAMES = 16
SHARED = 8
TCOLS = 4
TROWS = 4
TILES = TCOLS * TROWS
WINDOWS = 32
COLS = 20
C = 320
HALF = 256
PIX = COLS * FRAMES
WIDE = (COLS + 2) * FRAMES
MEMBERS = float(FRAMES * TILES * 2 * COLS * (C // GROUPS))


def pack_rest(field):
    half = field.shape[0] // 2
    return jnp.concatenate([field[:half, HALF:], field[half:, HALF:]], axis=1)


def unpack_rest(rest):
    return jnp.concatenate([rest[:, : C - HALF], rest[:, C - HALF :]], axis=0)


def exact_dot(rows, ones):
    high = rows.astype(BF16).astype(F32)
    rest = rows - high
    middle = rest.astype(BF16).astype(F32)
    low = rest - middle
    parts = jnp.concatenate([high, middle, low, jnp.zeros_like(low)], axis=0)
    product = jnp.dot(parts.astype(BF16), ones, preferred_element_type=F32)
    return product[0:2] + product[2:4] + product[4:6]


def silu(field):
    half = 0.5 * field
    return half + half * jnp.tanh(half)


def kernel(
    x_hbm, ws_hbm, wt_hbm, gain1, shift1, gain2, shift2, bias, starts, counts, out_ref,
    xv, xf, rows_m, rows_r, hrow_m, hrow_r, hcol, stat, stats, planes, acc, ws, wt, mixed,
    send_m, send_r, got_m, got_r,
    x_sem, w_sem, col_ssem, col_rsem, row_ssem, row_rsem, st_ssem, st_rsem, win_ssem, win_rsem,
):
    w = lax.axis_index("win")
    t = lax.axis_index("tile")
    r = t // TCOLS
    q = t % TCOLS
    up, down, left, right = r > 0, r < TROWS - 1, q > 0, q < TCOLS - 1
    first, last = w == 0, w == WINDOWS - 1

    x_copies = [
        pltpu.make_async_copy(x_hbm.at[:, c], xv.at[c], x_sem.at[c]) for c in range(COLS)
    ]
    for copy in x_copies:
        copy.start()
    ws_copy = pltpu.make_async_copy(ws_hbm, ws, w_sem.at[0])
    wt_copy = pltpu.make_async_copy(wt_hbm, wt, w_sem.at[1])
    ws_copy.start()
    wt_copy.start()

    barrier = pltpu.get_barrier_semaphore()
    peers = [(w, (t + i) % TILES) for i in range(1, TILES)]
    for peer in peers:
        pl.semaphore_signal(barrier, inc=1, device_id=peer, device_id_type=MESH)

    @pl.when(jnp.logical_not(first))
    def _():
        pl.semaphore_signal(barrier, inc=1, device_id=(w - 1, t), device_id_type=MESH)

    @pl.when(jnp.logical_not(last))
    def _():
        pl.semaphore_signal(barrier, inc=1, device_id=(w + 1, t), device_id_type=MESH)

    per = C // GROUPS
    group_of = lax.broadcasted_iota(jnp.int32, (C, 128), 0) // per
    to_groups = (group_of == lax.broadcasted_iota(jnp.int32, (C, 128), 1)).astype(F32).astype(BF16)
    channel_group = lax.broadcasted_iota(jnp.int32, (128, C), 1) // per
    to_channels = (
        (channel_group == lax.broadcasted_iota(jnp.int32, (128, C), 0)).astype(F32).astype(BF16)
    )

    for copy in x_copies:
        copy.wait()
    total = jnp.zeros((1, C), F32)
    square = jnp.zeros((1, C), F32)
    split = jnp.transpose(xv[...].reshape(PIX, 2, C).astype(F32), (1, 0, 2))
    for y in range(2):
        plane = split[y]
        xf[y] = plane
        rows_m[y] = plane[:, :HALF].astype(BF16)
        rows_r[y] = pack_rest(plane).astype(BF16)
        total = total + jnp.sum(plane, axis=0, keepdims=True)
        square = square + jnp.sum(plane * plane, axis=0, keepdims=True)
    stat[0] = exact_dot(jnp.concatenate([total, square], axis=0), to_groups)

    pl.semaphore_wait(
        barrier, TILES - 1 + jnp.where(first, 0, 1) + jnp.where(last, 0, 1)
    )

    def remote(src, dst, ssem, rsem, device):
        return pltpu.make_async_remote_copy(
            src_ref=src, dst_ref=dst, send_sem=ssem, recv_sem=rsem,
            device_id=device, device_id_type=MESH,
        )

    def stat_copies(which):
        return [
            remote(stat.at[which], stats.at[which, i], st_ssem.at[which, i], st_rsem.at[which, i], peers[i])
            for i in range(TILES - 1)
        ]

    first_stats = stat_copies(0)
    for copy in first_stats:
        copy.start()

    lefts, rights = xv.at[0], xv.at[COLS - 1]
    col_plan = [
        (right, rights, 1, left),
        (left, lefts, -1, right),
        (right & down, rights, TCOLS + 1, left & up),
        (left & down, lefts, TCOLS - 1, right & up),
        (right & up, rights, 1 - TCOLS, left & down),
        (left & up, lefts, -1 - TCOLS, right & down),
    ]
    col_copies = [
        remote(src, hcol.at[i], col_ssem.at[i], col_rsem.at[i], (w, (t + by + TILES) % TILES))
        for i, (_, src, by, _) in enumerate(col_plan)
    ]
    row_plan = [(down, 1, TCOLS, up), (up, 0, -TCOLS, down)]
    row_copies = [
        (
            remote(rows_m.at[y], hrow_m.at[i], row_ssem.at[i, 0], row_rsem.at[i, 0], (w, (t + by + TILES) % TILES)),
            remote(rows_r.at[y], hrow_r.at[i], row_ssem.at[i, 1], row_rsem.at[i, 1], (w, (t + by + TILES) % TILES)),
        )
        for i, (_, y, by, _) in enumerate(row_plan)
    ]

    def guarded(condition, *actions):
        @pl.when(condition)
        def _():
            for action in actions:
                action()

    for (sends, _, _, _), copy in zip(col_plan, col_copies):
        guarded(sends, copy.start)
    for (sends, _, _, _), pair in zip(row_plan, row_copies):
        guarded(sends, pair[0].start, pair[1].start)

    def finish_stats(which, copies):
        for copy in copies:
            copy.wait()
        totals = stat[which]
        for i in range(TILES - 1):
            totals = totals + stats[which, i]
        mean = totals[0:1] / MEMBERS
        spread = totals[1:2] / MEMBERS - mean * mean
        inverse = lax.rsqrt(spread + EPSILON)
        spread_out = exact_dot(jnp.concatenate([mean, inverse], axis=0), to_channels)
        return spread_out[0:1], spread_out[1:2]

    mean1, inverse1 = finish_stats(0, first_stats)
    scale1 = inverse1 * gain1[...]
    offset1 = shift1[...]

    def act(field):
        return silu((field - mean1) * scale1 + offset1).astype(BF16)

    for y in range(2):
        planes[1 + y, FRAMES : FRAMES + PIX] = act(xf[y])

    empty = jnp.zeros((FRAMES, C), BF16)
    places = [0, FRAMES * (COLS + 1)]
    for i in range(2):
        guarded(col_plan[i][3], col_copies[i].wait_recv)
        at = places[i]

        @pl.when(col_plan[i][3])
        def _(i=i, at=at):
            both = jnp.transpose(hcol[i].astype(F32), (1, 0, 2))
            for y in range(2):
                planes[1 + y, at : at + FRAMES] = act(both[y])

        @pl.when(jnp.logical_not(col_plan[i][3]))
        def _(at=at):
            for y in range(2):
                planes[1 + y, at : at + FRAMES] = empty

    for i in range(2, 6):
        guarded(col_plan[i][3], col_copies[i].wait_recv)
        at = places[i % 2]
        plane, y = (0, 1) if i < 4 else (3, 0)

        @pl.when(col_plan[i][3])
        def _(i=i, at=at, plane=plane, y=y):
            both = jnp.transpose(hcol[i].astype(F32), (1, 0, 2))
            planes[plane, at : at + FRAMES] = act(both[y])

        @pl.when(jnp.logical_not(col_plan[i][3]))
        def _(at=at, plane=plane):
            planes[plane, at : at + FRAMES] = empty

    ws_copy.wait()

    def taps(y, rows):
        summed = None
        for a in rows:
            for b in range(3):
                piece = planes[y + a, FRAMES * b : FRAMES * b + PIX]
                product = jnp.dot(piece, ws[a, b], preferred_element_type=F32)
                summed = product if summed is None else summed + product
        return summed

    acc[0] = taps(0, (1, 2))
    acc[1] = taps(1, (0, 1))

    for i in range(2):
        plane = 0 if i == 0 else 3

        @pl.when(row_plan[i][3])
        def _(i=i, plane=plane):
            row_copies[i][0].wait_recv()
            row_copies[i][1].wait_recv()
            arrived = jnp.concatenate(
                [hrow_m[i].astype(F32), unpack_rest(hrow_r[i].astype(F32))], axis=1
            )
            planes[plane, FRAMES : FRAMES + PIX] = act(arrived)

        @pl.when(jnp.logical_not(row_plan[i][3]))
        def _(plane=plane):
            planes[plane, FRAMES : FRAMES + PIX] = jnp.zeros((PIX, C), BF16)

    total = jnp.zeros((1, C), F32)
    square = jnp.zeros((1, C), F32)
    for y in range(2):
        spatial = (acc[y] + taps(y, (2 * y,))).astype(BF16).astype(F32)
        acc[y] = spatial
        total = total + jnp.sum(spatial, axis=0, keepdims=True)
        square = square + jnp.sum(spatial * spatial, axis=0, keepdims=True)
    stat[1] = exact_dot(jnp.concatenate([total, square], axis=0), to_groups)
    second_stats = stat_copies(1)
    for copy in second_stats:
        copy.start()

    lane_window = lax.broadcasted_iota(jnp.int32, (FRAMES, WINDOWS), 1)
    held = counts[...]

    def counts_of(index):
        return jnp.sum(jnp.where(lane_window == index, held, 0), axis=1, keepdims=True)

    start_lane = lax.broadcasted_iota(jnp.int32, (1, WINDOWS), 1)

    def start_of(index):
        return jnp.sum(jnp.where(start_lane == index, starts[...], 0), axis=1, keepdims=True)

    side = COLS * 2 // 5
    lane = lax.broadcasted_iota(jnp.int32, (side * FRAMES, side * FRAMES), 1)
    row = lax.broadcasted_iota(jnp.int32, (side * FRAMES, side * FRAMES), 0)
    frame = row % FRAMES
    from_prev = lane < side * SHARED
    slot = lane % SHARED
    same = row // FRAMES == (lane // SHARED) % side
    gap_prev = start_of(w) - start_of(w - 1)
    gap_next = start_of(w + 1) - start_of(w)
    wanted = jnp.where(from_prev, frame + gap_prev - (FRAMES - SHARED), frame - gap_next)
    exists = jnp.where(from_prev, jnp.where(first, 0, 1), jnp.where(last, 0, 1)) > 0
    lane16 = lax.broadcasted_iota(jnp.int32, (FRAMES, side * FRAMES), 1)
    frame16 = lax.broadcasted_iota(jnp.int32, (FRAMES, side * FRAMES), 0)
    prev_lanes = lane16 < side * SHARED
    at_frame = frame16 == lane16 % SHARED + jnp.where(prev_lanes, FRAMES - SHARED, 0)
    lane_counts = jnp.sum(
        jnp.where(at_frame, jnp.where(prev_lanes, counts_of(w - 1), counts_of(w + 1)), 0),
        axis=0,
        keepdims=True,
    )
    blend = jnp.where(same & exists & (slot == wanted), lane_counts, 0).astype(F32)
    own = jnp.concatenate([counts_of(w).astype(F32)] * side, axis=0)
    denominator = own + jnp.sum(blend, axis=1, keepdims=True)
    blend_matrix = blend.astype(BF16)

    mean2, inverse2 = finish_stats(1, second_stats)
    scale2 = inverse2 * gain2[...]
    offset2 = shift2[...]
    for y in range(2):
        mixed[y * PIX : (y + 1) * PIX] = silu((acc[y] - mean2) * scale2 + offset2).astype(BF16)

    wt_copy.wait()
    frame_at = lax.broadcasted_iota(jnp.int32, (PIX, 1), 0) % FRAMES
    blocks = []
    for y in range(2):
        piece = mixed[y * PIX : (y + 1) * PIX]
        running = xf[y] + bias[...] + jnp.dot(piece, wt[1], preferred_element_type=F32)
        before = jnp.dot(piece, wt[0], preferred_element_type=F32)
        running = running + jnp.where(frame_at > 0, pltpu.roll(before, 1, 0), 0.0)
        after = jnp.dot(piece, wt[2], preferred_element_type=F32)
        running = running + jnp.where(frame_at < FRAMES - 1, pltpu.roll(after, PIX - 1, 0), 0.0)
        block = running.astype(BF16).astype(F32)
        acc[y] = block
        halves = block.reshape(COLS, 2, SHARED, C)
        for part in range(2):
            dense = halves[:, part].reshape(COLS * SHARED, C)
            send_m[part, y * COLS * SHARED : (y + 1) * COLS * SHARED] = dense[:, :HALF].astype(BF16)
            half = COLS * SHARED // 2
            send_r[part, y * half : (y + 1) * half] = pack_rest(dense).astype(BF16)

    head = (
        remote(send_m.at[0], got_m.at[1], win_ssem.at[0, 0], win_rsem.at[0, 0], (lax.max(w - 1, 0), t)),
        remote(send_r.at[0], got_r.at[1], win_ssem.at[0, 1], win_rsem.at[0, 1], (lax.max(w - 1, 0), t)),
    )
    tail = (
        remote(send_m.at[1], got_m.at[0], win_ssem.at[1, 0], win_rsem.at[1, 0], (lax.min(w + 1, WINDOWS - 1), t)),
        remote(send_r.at[1], got_r.at[0], win_ssem.at[1, 1], win_rsem.at[1, 1], (lax.min(w + 1, WINDOWS - 1), t)),
    )
    has_prev, has_next = jnp.logical_not(first), jnp.logical_not(last)
    guarded(has_prev, head[0].start, head[1].start)
    guarded(has_next, tail[0].start, tail[1].start)

    @pl.when(first)
    def _():
        got_m[0] = jnp.zeros((PIX, HALF), BF16)
        got_r[0] = jnp.zeros((PIX // 2, 128), BF16)

    @pl.when(last)
    def _():
        got_m[1] = jnp.zeros((PIX, HALF), BF16)
        got_r[1] = jnp.zeros((PIX // 2, 128), BF16)

    for (sends, _, _, _), copy in zip(col_plan, col_copies):
        guarded(sends, copy.wait_send)
    for (sends, _, _, _), pair in zip(row_plan, row_copies):
        guarded(sends, pair[0].wait_send, pair[1].wait_send)
    guarded(has_prev, tail[0].wait_recv, tail[1].wait_recv)
    guarded(has_next, head[0].wait_recv, head[1].wait_recv)
    guarded(has_prev, head[0].wait_send, head[1].wait_send)
    guarded(has_next, tail[0].wait_send, tail[1].wait_send)

    share = 1.0 / denominator
    depth = side * SHARED
    half = COLS * SHARED // 2

    def whole(part):
        rests = [unpack_rest(got_r[part, y * half : (y + 1) * half].astype(F32)) for y in range(2)]
        rest = jnp.concatenate(rests, axis=0).astype(BF16)
        return jnp.concatenate([got_m[part], rest], axis=1)

    prev_all, next_all = whole(0), whole(1)
    own_all = acc[...].reshape(2 * PIX, C)
    joined = []
    for k in range(5):
        others = jnp.concatenate(
            [prev_all[k * depth : (k + 1) * depth], next_all[k * depth : (k + 1) * depth]], axis=0
        )
        numerator = jnp.dot(blend_matrix, others, preferred_element_type=F32)
        numerator = numerator + own * own_all[k * side * FRAMES : (k + 1) * side * FRAMES]
        joined.append(numerator * share)
    result = jnp.concatenate(joined, axis=0).reshape(2, PIX, C)
    both = jnp.stack([result[0], result[1]], axis=1).astype(BF16)
    out_ref[...] = both.reshape(COLS, FRAMES, 2, C)


def on_device(
    latents, spatial_weight, temporal_weight, gain_first, shift_first, gain_second, shift_second,
    temporal_bias, starts, blend_counts,
):
    x = jnp.transpose(latents.reshape(FRAMES, 2, COLS, C), (0, 2, 1, 3))
    vmem = pl.BlockSpec(memory_space=pltpu.VMEM)
    hbm = pl.BlockSpec(memory_space=pl.ANY)
    dma = pltpu.SemaphoreType.DMA
    out = pl.pallas_call(
        kernel,
        out_shape=jax.ShapeDtypeStruct((COLS, FRAMES, 2, C), BF16),
        in_specs=[hbm] * 3 + [vmem] * 7,
        out_specs=vmem,
        scratch_shapes=[
            pltpu.VMEM((COLS, FRAMES, 2, C), BF16),
            pltpu.VMEM((2, PIX, C), F32),
            pltpu.VMEM((2, PIX, HALF), BF16),
            pltpu.VMEM((2, PIX // 2, 128), BF16),
            pltpu.VMEM((2, PIX, HALF), BF16),
            pltpu.VMEM((2, PIX // 2, 128), BF16),
            pltpu.VMEM((6, FRAMES, 2, C), BF16),
            pltpu.VMEM((2, 2, 128), F32),
            pltpu.VMEM((2, TILES - 1, 2, 128), F32),
            pltpu.VMEM((4, WIDE, C), BF16),
            pltpu.VMEM((2, PIX, C), F32),
            pltpu.VMEM((3, 3, C, C), BF16),
            pltpu.VMEM((3, C, C), BF16),
            pltpu.VMEM((2 * PIX, C), BF16),
            pltpu.VMEM((2, PIX, HALF), BF16),
            pltpu.VMEM((2, PIX // 2, 128), BF16),
            pltpu.VMEM((2, PIX, HALF), BF16),
            pltpu.VMEM((2, PIX // 2, 128), BF16),
            dma((COLS,)),
            dma((2,)),
            dma((6,)),
            dma((6,)),
            dma((2, 2)),
            dma((2, 2)),
            dma((2, TILES - 1)),
            dma((2, TILES - 1)),
            dma((2, 2)),
            dma((2, 2)),
        ],
        compiler_params=pltpu.CompilerParams(
            collective_id=0, has_side_effects=True, vmem_limit_bytes=48 << 20
        ),
        cost_estimate=pl.CostEstimate(flops=1_600_000_000, bytes_accessed=4_000_000, transcendentals=400_000),
        name="resblock",
    )(
        x, spatial_weight, temporal_weight, gain_first.reshape(1, C), shift_first.reshape(1, C),
        gain_second.reshape(1, C), shift_second.reshape(1, C), temporal_bias.reshape(1, C),
        starts.reshape(1, WINDOWS), blend_counts.T,
    )
    return jnp.transpose(out, (1, 2, 0, 3)).reshape(1, FRAMES, 1, 2, COLS, C)


def solution(mesh):
    return jax.shard_map(
        on_device,
        mesh=mesh,
        in_specs=(P("win", None, "tile", None, None, None),) + (P(),) * 9,
        out_specs=P("win", None, "tile", None, None, None),
        check_vma=False,
    )
```

time: 204 us -> 73.2 us (0.36)
  the two profiles are of different devices: /device:TPU:24 before, /device:TPU:56 now
where the time goes in v1:
time: 73.2 us; the launch traced here: 72.7 us
  Pallas kernels  63 us (86%)
  local copies, waits for them, and re-layouts  9.65 us (13%)
    pallas_call x1, Pallas kernels, on_device(): pl.pallas_call(kernel, out_shape=jax.ShapeDtypeStruct((COLS, FRAMES, 2, C...  63 us
    unnamed x10, local copies, waits for them, and re-layouts  5.12 us

profile of v1, /device:TPU:56, one launch (start us, length us, event | category | flops | bytes accessed | tf_op | source)
XLA Modules:
  0.0 72.7 jit_solution(11382021056912504672)
XLA Ops:
  0.0 0.7 reshape.25.gain1
  0.7 0.7 reshape.26.shift1
  1.4 0.7 reshape.27.gain2
  2.0 0.7 reshape.28.shift2
  2.7 0.7 reshape.29.bias
  3.4 0.0 copy-start
  3.4 1.6 %copy-done = bf16[3,3,320,320]{3,2,1,0:T(8,128)(2,1)S(1)} copy-done((bf16[3,3,320,320]{3,2,1,0:T(8,128)(2,1)S(1)}, bf16[3,3,320,320]{3,2,1,0:T(8,128)(2,1)}, u32[]{:S(2)}) %copy-start) | copy-done | bytes 1843224
  5.0 0.0 copy-start.1
  5.0 1.1 %copy-done.1 = bf16[3,320,320]{2,1,0:T(8,128)(2,1)S(1)} copy-done((bf16[3,320,320]{2,1,0:T(8,128)(2,1)S(1)}, bf16[3,320,320]{2,1,0:T(8,128)(2,1)}, u32[]{:S(2)}) %copy-start.1) | copy-done | bytes 614424
  6.2 0.0 copy-start.2
  6.2 1.0 %copy-done.2 = bf16[1,16,1,2,20,320]{5,3,4,2,1,0:T(2,128)(2,1)S(1)} copy-done((bf16[1,16,1,2,20,320]{5,3,4,2,1,0:T(2,128)(2,1)S(1)}, bf16[1,16,1,2,20,320]{5,3,4,2,1,0:T(2,128)(2,1)}, u32[]{:S(2)}) %copy-start.2) | copy-done | bytes 409624
  7.2 0.0 copy-start.3
  7.2 0.7 copy-done.3
  7.9 0.0 copy-start.4
  7.9 0.7 copy-done.4
  8.5 63.0 %resblock.1 = bf16[20,16,2,320]{3,2,1,0:T(2,128)(2,1)S(1)} custom-call(bf16[16,20,2,320]{3,2,1,0:T(2,128)(2,1)S(1)} %bitcast.9, bf16[3,3,320,320]{3,2,1,0:T(8,128)(2,1)S(1)} %copy-done, bf16[3,320,320]{2,1,0:T(8,128)(2,1)S(1)} %copy-done.1, f32[1,320]{1,0:T(1,128)S(1)} %reshape.25.gain1, f32[1,320]{1,0:T(1,128)S(1)} %reshape.26.shift1, ...), custom_call_target="tpu_custom_call" | custom-call | flops 1600000000 | bytes 4000000 | tf_op jit(solution)/shard_map/resblock/pallas_call | solution.py:382
  71.6 1.1 %copy.11 = bf16[1,16,1,2,20,320]{5,3,4,2,1,0:T(2,128)(2,1)} copy(bf16[1,16,1,2,20,320]{5,3,1,4,2,0:T(2,128)(2,1)S(1)} %bitcast.8) | data formatting | bytes 819200 | tf_op jit(solution)/shard_map/reshape | solution.py:427
Async XLA Ops:
  3.4 1.6 %copy-start = (bf16[3,3,320,320]{3,2,1,0:T(8,128)(2,1)S(1)}, bf16[3,3,320,320]{3,2,1,0:T(8,128)(2,1)}, u32[]{:S(2)}) copy-start(bf16[3,3,320,320]{3,2,1,0:T(8,128)(2,1)} %ws_hbm.1) | copy-start | bytes 5529604
  5.0 1.1 %copy-start.1 = (bf16[3,320,320]{2,1,0:T(8,128)(2,1)S(1)}, bf16[3,320,320]{2,1,0:T(8,128)(2,1)}, u32[]{:S(2)}) copy-start(bf16[3,320,320]{2,1,0:T(8,128)(2,1)} %wt_hbm.1) | copy-start | bytes 1843204
  6.2 1.0 %copy-start.2 = (bf16[1,16,1,2,20,320]{5,3,4,2,1,0:T(2,128)(2,1)S(1)}, bf16[1,16,1,2,20,320]{5,3,4,2,1,0:T(2,128)(2,1)}, u32[]{:S(2)}) copy-start(bf16[1,16,1,2,20,320]{5,3,4,2,1,0:T(2,128)(2,1)} %param.10) | copy-start | bytes 1228804
  7.2 0.7 copy-start.3
  7.9 0.7 copy-start.4

commit v2 on v1

--- a/solution.py
+++ b/solution.py
@@ -19,19 +19,28 @@
 WINDOWS = 32
 COLS = 20
 C = 320
-HALF = 256
+LANES = 128
 PIX = COLS * FRAMES
 WIDE = (COLS + 2) * FRAMES
+PACKED = PIX * 5 // 2
+SIDE = 8
+FIRST = 2 * SIDE * SHARED
+SECOND = 3 * SIDE * SHARED
 MEMBERS = float(FRAMES * TILES * 2 * COLS * (C // GROUPS))
 
 
-def pack_rest(field):
+def pack(field):
     half = field.shape[0] // 2
-    return jnp.concatenate([field[:half, HALF:], field[half:, HALF:]], axis=1)
-
-
-def unpack_rest(rest):
-    return jnp.concatenate([rest[:, : C - HALF], rest[:, C - HALF :]], axis=0)
+    rest = jnp.concatenate([field[:half, 2 * LANES :], field[half:, 2 * LANES :]], axis=1)
+    return jnp.concatenate([field[:, :LANES], field[:, LANES : 2 * LANES], rest], axis=0)
+
+
+def unpack(packed):
+    n = packed.shape[0] * 2 // 5
+    rest = packed[2 * n :]
+    tail = C - 2 * LANES
+    rest = jnp.concatenate([rest[:, :tail], rest[:, tail:]], axis=0)
+    return jnp.concatenate([packed[:n], packed[n : 2 * n], rest], axis=1)
 
 
 def exact_dot(rows, ones):
@@ -50,10 +59,10 @@
 
 
 def kernel(
-    x_hbm, ws_hbm, wt_hbm, gain1, shift1, gain2, shift2, bias, starts, counts, out_ref,
-    xv, xf, rows_m, rows_r, hrow_m, hrow_r, hcol, stat, stats, planes, acc, ws, wt, mixed,
-    send_m, send_r, got_m, got_r,
-    x_sem, w_sem, col_ssem, col_rsem, row_ssem, row_rsem, st_ssem, st_rsem, win_ssem, win_rsem,
+    x_hbm, ws_hbm, wt_hbm, gain1_hbm, shift1_hbm, gain2_hbm, shift2_hbm, bias_hbm, starts_hbm, counts_hbm, out_ref,
+    xv, xf, rows, hrow, hcol, stat, stats, planes, acc, ws, wt, mixed,
+    send_a, send_b, got_a, got_b, passing,
+    gain1, shift1, gain2, shift2, bias, starts, counts, x_sem, w_sem, small_sem, col_ssem, col_rsem, row_ssem, row_rsem, st_ssem, st_rsem, win_ssem, win_rsem, pass_ssem, pass_rsem,
 ):
     w = lax.axis_index("win")
     t = lax.axis_index("tile")
@@ -61,6 +70,12 @@
     q = t % TCOLS
     up, down, left, right = r > 0, r < TROWS - 1, q > 0, q < TCOLS - 1
     first, last = w == 0, w == WINDOWS - 1
+    x = w % 4
+    has_prev, has_next = w > 0, w < WINDOWS - 1
+    far_next = (x == 3) & has_next
+    far_prev = (x == 0) & has_prev
+    relay_up = (x == 2) & (w + 2 < WINDOWS)
+    relay_down = (x == 1) & (w - 2 >= 0)
 
     x_copies = [
         pltpu.make_async_copy(x_hbm.at[:, c], xv.at[c], x_sem.at[c]) for c in range(COLS)
@@ -72,18 +87,30 @@
     ws_copy.start()
     wt_copy.start()
 
+    small = [(gain1_hbm, gain1), (shift1_hbm, shift1), (gain2_hbm, gain2), (shift2_hbm, shift2),
+             (bias_hbm, bias), (starts_hbm, starts), (counts_hbm, counts)]
+    small_copies = [
+        pltpu.make_async_copy(src, dst, small_sem.at[i]) for i, (src, dst) in enumerate(small)
+    ]
+    for copy in small_copies:
+        copy.start()
+
     barrier = pltpu.get_barrier_semaphore()
     peers = [(w, (t + i) % TILES) for i in range(1, TILES)]
     for peer in peers:
         pl.semaphore_signal(barrier, inc=1, device_id=peer, device_id_type=MESH)
 
-    @pl.when(jnp.logical_not(first))
-    def _():
-        pl.semaphore_signal(barrier, inc=1, device_id=(w - 1, t), device_id_type=MESH)
-
-    @pl.when(jnp.logical_not(last))
-    def _():
-        pl.semaphore_signal(barrier, inc=1, device_id=(w + 1, t), device_id_type=MESH)
+    greets = [
+        (has_prev, w - 1),
+        (has_next, w + 1),
+        (relay_up | far_next, w + 2),
+        (relay_down | far_prev, w - 2),
+    ]
+    for condition, other in greets:
+
+        @pl.when(condition)
+        def _(other=other):
+            pl.semaphore_signal(barrier, inc=1, device_id=(other, t), device_id_type=MESH)
 
     per = C // GROUPS
     group_of = lax.broadcasted_iota(jnp.int32, (C, 128), 0) // per
@@ -101,14 +128,13 @@
     for y in range(2):
         plane = split[y]
         xf[y] = plane
-        rows_m[y] = plane[:, :HALF].astype(BF16)
-        rows_r[y] = pack_rest(plane).astype(BF16)
+        rows[y] = pack(plane).astype(BF16)
         total = total + jnp.sum(plane, axis=0, keepdims=True)
         square = square + jnp.sum(plane * plane, axis=0, keepdims=True)
     stat[0] = exact_dot(jnp.concatenate([total, square], axis=0), to_groups)
 
     pl.semaphore_wait(
-        barrier, TILES - 1 + jnp.where(first, 0, 1) + jnp.where(last, 0, 1)
+        barrier, TILES - 1 + sum(jnp.where(condition, 1, 0) for condition, _ in greets)
     )
 
     def remote(src, dst, ssem, rsem, device):
@@ -142,10 +168,7 @@
     ]
     row_plan = [(down, 1, TCOLS, up), (up, 0, -TCOLS, down)]
     row_copies = [
-        (
-            remote(rows_m.at[y], hrow_m.at[i], row_ssem.at[i, 0], row_rsem.at[i, 0], (w, (t + by + TILES) % TILES)),
-            remote(rows_r.at[y], hrow_r.at[i], row_ssem.at[i, 1], row_rsem.at[i, 1], (w, (t + by + TILES) % TILES)),
-        )
+        remote(rows.at[y], hrow.at[i], row_ssem.at[i], row_rsem.at[i], (w, (t + by + TILES) % TILES))
         for i, (_, y, by, _) in enumerate(row_plan)
     ]
 
@@ -157,8 +180,8 @@
 
     for (sends, _, _, _), copy in zip(col_plan, col_copies):
         guarded(sends, copy.start)
-    for (sends, _, _, _), pair in zip(row_plan, row_copies):
-        guarded(sends, pair[0].start, pair[1].start)
+    for (sends, _, _, _), copy in zip(row_plan, row_copies):
+        guarded(sends, copy.start)
 
     def finish_stats(which, copies):
         for copy in copies:
@@ -173,8 +196,10 @@
         return spread_out[0:1], spread_out[1:2]
 
     mean1, inverse1 = finish_stats(0, first_stats)
-    scale1 = inverse1 * gain1[...]
-    offset1 = shift1[...]
+    for copy in small_copies:
+        copy.wait()
+    scale1 = inverse1 * gain1[...].reshape(1, C)
+    offset1 = shift1[...].reshape(1, C)
 
     def act(field):
         return silu((field - mean1) * scale1 + offset1).astype(BF16)
@@ -232,12 +257,8 @@
 
         @pl.when(row_plan[i][3])
         def _(i=i, plane=plane):
-            row_copies[i][0].wait_recv()
-            row_copies[i][1].wait_recv()
-            arrived = jnp.concatenate(
-                [hrow_m[i].astype(F32), unpack_rest(hrow_r[i].astype(F32))], axis=1
-            )
-            planes[plane, FRAMES : FRAMES + PIX] = act(arrived)
+            row_copies[i].wait_recv()
+            planes[plane, FRAMES : FRAMES + PIX] = act(unpack(hrow[i].astype(F32)))
 
         @pl.when(jnp.logical_not(row_plan[i][3]))
         def _(plane=plane):
@@ -264,9 +285,9 @@
     start_lane = lax.broadcasted_iota(jnp.int32, (1, WINDOWS), 1)
 
     def start_of(index):
-        return jnp.sum(jnp.where(start_lane == index, starts[...], 0), axis=1, keepdims=True)
-
-    side = COLS * 2 // 5
+        return jnp.sum(jnp.where(start_lane == index, starts[...].reshape(1, WINDOWS), 0), axis=1, keepdims=True)
+
+    side = SIDE
     lane = lax.broadcasted_iota(jnp.int32, (side * FRAMES, side * FRAMES), 1)
     row = lax.broadcasted_iota(jnp.int32, (side * FRAMES, side * FRAMES), 0)
     frame = row % FRAMES
@@ -292,17 +313,48 @@
     blend_matrix = blend.astype(BF16)
 
     mean2, inverse2 = finish_stats(1, second_stats)
-    scale2 = inverse2 * gain2[...]
-    offset2 = shift2[...]
+    scale2 = inverse2 * gain2[...].reshape(1, C)
+    offset2 = shift2[...].reshape(1, C)
     for y in range(2):
         mixed[y * PIX : (y + 1) * PIX] = silu((acc[y] - mean2) * scale2 + offset2).astype(BF16)
 
     wt_copy.wait()
     frame_at = lax.broadcasted_iota(jnp.int32, (PIX, 1), 0) % FRAMES
-    blocks = []
+    def window(index):
+        return (lax.clamp(0, index, WINDOWS - 1), t)
+
+    direct_a = [
+        remote(send_a.at[0], got_a.at[1], win_ssem.at[0, 0], win_rsem.at[0, 0], window(w - 1)),
+        remote(send_a.at[1], got_a.at[0], win_ssem.at[1, 0], win_rsem.at[1, 0], window(w + 1)),
+    ]
+    direct_b = [
+        remote(send_b.at[0], got_b.at[1], win_ssem.at[0, 1], win_rsem.at[0, 1], window(w - 1)),
+        remote(send_b.at[1], got_b.at[0], win_ssem.at[1, 1], win_rsem.at[1, 1], window(w + 1)),
+    ]
+    aside = [
+        remote(send_a.at[0], passing, win_ssem.at[0, 0], pass_rsem.at[0], window(w + 1)),
+        remote(send_a.at[1], passing, win_ssem.at[1, 0], pass_rsem.at[0], window(w - 1)),
+    ]
+    onward = [
+        remote(passing, got_a.at[1], pass_ssem.at[0], win_rsem.at[0, 0], window(w - 2)),
+        remote(passing, got_a.at[0], pass_ssem.at[0], win_rsem.at[1, 0], window(w + 2)),
+    ]
+
+    @pl.when(first)
+    def _():
+        got_a[0] = jnp.zeros_like(got_a[0])
+        got_b[0] = jnp.zeros_like(got_b[0])
+
+    @pl.when(last)
+    def _():
+        got_a[1] = jnp.zeros_like(got_a[1])
+        got_b[1] = jnp.zeros_like(got_b[1])
+
+    frame_rows = COLS * SHARED
+    left_over = []
     for y in range(2):
         piece = mixed[y * PIX : (y + 1) * PIX]
-        running = xf[y] + bias[...] + jnp.dot(piece, wt[1], preferred_element_type=F32)
+        running = xf[y] + bias[...].reshape(1, C) + jnp.dot(piece, wt[1], preferred_element_type=F32)
         before = jnp.dot(piece, wt[0], preferred_element_type=F32)
         running = running + jnp.where(frame_at > 0, pltpu.roll(before, 1, 0), 0.0)
         after = jnp.dot(piece, wt[2], preferred_element_type=F32)
@@ -311,50 +363,38 @@
         acc[y] = block
         halves = block.reshape(COLS, 2, SHARED, C)
         for part in range(2):
-            dense = halves[:, part].reshape(COLS * SHARED, C)
-            send_m[part, y * COLS * SHARED : (y + 1) * COLS * SHARED] = dense[:, :HALF].astype(BF16)
-            half = COLS * SHARED // 2
-            send_r[part, y * half : (y + 1) * half] = pack_rest(dense).astype(BF16)
-
-    head = (
-        remote(send_m.at[0], got_m.at[1], win_ssem.at[0, 0], win_rsem.at[0, 0], (lax.max(w - 1, 0), t)),
-        remote(send_r.at[0], got_r.at[1], win_ssem.at[0, 1], win_rsem.at[0, 1], (lax.max(w - 1, 0), t)),
-    )
-    tail = (
-        remote(send_m.at[1], got_m.at[0], win_ssem.at[1, 0], win_rsem.at[1, 0], (lax.min(w + 1, WINDOWS - 1), t)),
-        remote(send_r.at[1], got_r.at[0], win_ssem.at[1, 1], win_rsem.at[1, 1], (lax.min(w + 1, WINDOWS - 1), t)),
-    )
-    has_prev, has_next = jnp.logical_not(first), jnp.logical_not(last)
-    guarded(has_prev, head[0].start, head[1].start)
-    guarded(has_next, tail[0].start, tail[1].start)
-
-    @pl.when(first)
-    def _():
-        got_m[0] = jnp.zeros((PIX, HALF), BF16)
-        got_r[0] = jnp.zeros((PIX // 2, 128), BF16)
-
-    @pl.when(last)
-    def _():
-        got_m[1] = jnp.zeros((PIX, HALF), BF16)
-        got_r[1] = jnp.zeros((PIX // 2, 128), BF16)
+            dense = halves[:, part].reshape(frame_rows, C)
+            if y == 0:
+                send_a[part] = pack(dense[:FIRST]).astype(BF16)
+                left_over.append(dense[FIRST:])
+            else:
+                send_b[part] = pack(jnp.concatenate([left_over[part], dense], axis=0)).astype(BF16)
+        if y == 0:
+            guarded(has_prev & jnp.logical_not(far_prev), direct_a[0].start)
+            guarded(has_next & jnp.logical_not(far_next), direct_a[1].start)
+            guarded(far_prev, aside[0].start)
+            guarded(far_next, aside[1].start)
+    guarded(has_prev, direct_b[0].start)
+    guarded(has_next, direct_b[1].start)
+    guarded(relay_down, aside[0].wait_recv, onward[0].start)
+    guarded(relay_up, aside[1].wait_recv, onward[1].start)
 
     for (sends, _, _, _), copy in zip(col_plan, col_copies):
         guarded(sends, copy.wait_send)
-    for (sends, _, _, _), pair in zip(row_plan, row_copies):
-        guarded(sends, pair[0].wait_send, pair[1].wait_send)
-    guarded(has_prev, tail[0].wait_recv, tail[1].wait_recv)
-    guarded(has_next, head[0].wait_recv, head[1].wait_recv)
-    guarded(has_prev, head[0].wait_send, head[1].wait_send)
-    guarded(has_next, tail[0].wait_send, tail[1].wait_send)
+    for (sends, _, _, _), copy in zip(row_plan, row_copies):
+        guarded(sends, copy.wait_send)
+    guarded(has_prev, direct_a[1].wait_recv, direct_b[1].wait_recv)
+    guarded(has_next, direct_a[0].wait_recv, direct_b[0].wait_recv)
+    guarded(has_prev, direct_a[0].wait_send, direct_b[0].wait_send)
+    guarded(has_next, direct_a[1].wait_send, direct_b[1].wait_send)
+    guarded(relay_down, onward[0].wait_send)
+    guarded(relay_up, onward[1].wait_send)
 
     share = 1.0 / denominator
     depth = side * SHARED
-    half = COLS * SHARED // 2
 
     def whole(part):
-        rests = [unpack_rest(got_r[part, y * half : (y + 1) * half].astype(F32)) for y in range(2)]
-        rest = jnp.concatenate(rests, axis=0).astype(BF16)
-        return jnp.concatenate([got_m[part], rest], axis=1)
+        return jnp.concatenate([unpack(got_a[part]), unpack(got_b[part])], axis=0)
 
     prev_all, next_all = whole(0), whole(1)
     own_all = acc[...].reshape(2 * PIX, C)
@@ -377,20 +417,18 @@
 ):
     x = jnp.transpose(latents.reshape(FRAMES, 2, COLS, C), (0, 2, 1, 3))
     vmem = pl.BlockSpec(memory_space=pltpu.VMEM)
-    hbm = pl.BlockSpec(memory_space=pl.ANY)
+    hbm = pl.BlockSpec(memory_space=pltpu.HBM)
     dma = pltpu.SemaphoreType.DMA
     out = pl.pallas_call(
         kernel,
         out_shape=jax.ShapeDtypeStruct((COLS, FRAMES, 2, C), BF16),
-        in_specs=[hbm] * 3 + [vmem] * 7,
+        in_specs=[hbm] * 10,
         out_specs=vmem,
         scratch_shapes=[
             pltpu.VMEM((COLS, FRAMES, 2, C), BF16),
             pltpu.VMEM((2, PIX, C), F32),
-            pltpu.VMEM((2, PIX, HALF), BF16),
-            pltpu.VMEM((2, PIX // 2, 128), BF16),
-            pltpu.VMEM((2, PIX, HALF), BF16),
-            pltpu.VMEM((2, PIX // 2, 128), BF16),
+            pltpu.VMEM((2, PACKED, LANES), BF16),
+            pltpu.VMEM((2, PACKED, LANES), BF16),
             pltpu.VMEM((6, FRAMES, 2, C), BF16),
             pltpu.VMEM((2, 2, 128), F32),
             pltpu.VMEM((2, TILES - 1, 2, 128), F32),
@@ -399,30 +437,40 @@
             pltpu.VMEM((3, 3, C, C), BF16),
             pltpu.VMEM((3, C, C), BF16),
             pltpu.VMEM((2 * PIX, C), BF16),
-            pltpu.VMEM((2, PIX, HALF), BF16),
-            pltpu.VMEM((2, PIX // 2, 128), BF16),
-            pltpu.VMEM((2, PIX, HALF), BF16),
-            pltpu.VMEM((2, PIX // 2, 128), BF16),
+            pltpu.VMEM((2, FIRST * 5 // 2, LANES), BF16),
+            pltpu.VMEM((2, SECOND * 5 // 2, LANES), BF16),
+            pltpu.VMEM((2, FIRST * 5 // 2, LANES), BF16),
+            pltpu.VMEM((2, SECOND * 5 // 2, LANES), BF16),
+            pltpu.VMEM((FIRST * 5 // 2, LANES), BF16),
+            pltpu.VMEM((C,), F32),
+            pltpu.VMEM((C,), F32),
+            pltpu.VMEM((C,), F32),
+            pltpu.VMEM((C,), F32),
+            pltpu.VMEM((C,), F32),
+            pltpu.VMEM((WINDOWS,), jnp.int32),
+            pltpu.VMEM((FRAMES, WINDOWS), jnp.int32),
             dma((COLS,)),
             dma((2,)),
+            dma((7,)),
             dma((6,)),
             dma((6,)),
-            dma((2, 2)),
-            dma((2, 2)),
+            dma((2,)),
+            dma((2,)),
             dma((2, TILES - 1)),
             dma((2, TILES - 1)),
             dma((2, 2)),
             dma((2, 2)),
+            dma((1,)),
+            dma((1,)),
         ],
         compiler_params=pltpu.CompilerParams(
-            collective_id=0, has_side_effects=True, vmem_limit_bytes=48 << 20
+            collective_id=0, has_side_effects=True, vmem_limit_bytes=60 << 20
         ),
         cost_estimate=pl.CostEstimate(flops=1_600_000_000, bytes_accessed=4_000_000, transcendentals=400_000),
         name="resblock",
     )(
-        x, spatial_weight, temporal_weight, gain_first.reshape(1, C), shift_first.reshape(1, C),
-        gain_second.reshape(1, C), shift_second.reshape(1, C), temporal_bias.reshape(1, C),
-        starts.reshape(1, WINDOWS), blend_counts.T,
+        x, spatial_weight, temporal_weight, gain_first, shift_first, gain_second, shift_second,
+        temporal_bias, starts, blend_counts.T,
     )
     return jnp.transpose(out, (1, 2, 0, 3)).reshape(1, FRAMES, 1, 2, COLS, C)
 

time: 73.2 us -> 60 us (0.82)
  local copies, waits for them, and re-layouts: 9.65 us -> 2.15 us
  Pallas kernels: 63 us -> 57.7 us
    pallas_call x1, Pallas kernels: 63 us -> 57.7 us  [on_device(): pl.pallas_call(kernel, out_shape=jax.ShapeDtypeStruct((COLS, FRAMES, 2, C...]
    unnamed x10 -> x0, local copies, waits for them, and re-layouts: 5.12 us -> none
    reshape x5 -> x0, local copies, waits for them, and re-layouts: 3.41 us -> none  [the longest x1 0.68 us: on_device(): gain_first.reshape(1, C)]
    reshape x1, local copies, waits for them, and re-layouts: 1.12 us -> 2.15 us  [on_device(): return jnp.transpose(out, (1, 2, 0, 3)).reshape(1, FRAMES, 1, 2, COLS, C)]
where the time goes in v2:
time: 60 us; the launch traced here: 59.8 us
  Pallas kernels  57.7 us (96%)
  local copies, waits for them, and re-layouts  2.15 us (4%)
    pallas_call x1, Pallas kernels, on_device(): pl.pallas_call(kernel, out_shape=jax.ShapeDtypeStruct((COLS, FRAMES, 2, C...  57.7 us
    reshape x1, local copies, waits for them, and re-layouts, on_device(): return jnp.transpose(out, (1, 2, 0, 3)).reshape(1, FRAMES, 1, 2, COLS, C)  2.15 us

profile of v2, /device:TPU:56, one launch (start us, length us, event | category | flops | bytes accessed | tf_op | source)
XLA Modules:
  0.0 59.8 jit_solution(18358714591010325252)
XLA Ops:
  0.0 57.7 %resblock.1 = bf16[20,16,2,320]{3,2,1,0:T(2,128)(2,1)} custom-call(bf16[16,20,2,320]{3,2,1,0:T(2,128)(2,1)} %bitcast.8, bf16[3,3,320,320]{3,2,1,0:T(8,128)(2,1)} %ws_hbm.1, bf16[3,320,320]{2,1,0:T(8,128)(2,1)} %wt_hbm.1, f32[320]{0:T(512)} %gain1_hbm.1, f32[320]{0:T(512)} %shift1_hbm.1, f32[320]{0:T(512)} %gain2_hbm.1, f32[320]{0:T(512)} %shift2_hbm.1, ...), custom_call_target="tpu_custom_call" | custom-call | flops 1600000000 | bytes 4000000 | tf_op jit(solution)/shard_map/resblock/pallas_call | solution.py:422
  57.7 2.1 %copy.11 = bf16[1,16,1,2,20,320]{5,3,4,2,1,0:T(2,128)(2,1)} copy(bf16[1,16,1,2,20,320]{5,3,1,4,2,0:T(2,128)(2,1)} %bitcast.7) | data formatting | bytes 819200 | tf_op jit(solution)/shard_map/reshape | solution.py:475

commit v3 on v2

--- a/solution.py
+++ b/solution.py
@@ -24,8 +24,11 @@
 WIDE = (COLS + 2) * FRAMES
 PACKED = PIX * 5 // 2
 SIDE = 8
-FIRST = 2 * SIDE * SHARED
-SECOND = 3 * SIDE * SHARED
+CHUNKS = (64, 64, 192)
+PASSED = 2
+STARTS = tuple(sum(CHUNKS[:i]) for i in range(len(CHUNKS) + 1))
+ROW_CHUNKS = (64, 256)
+ROW_STARTS = (0, 64, 320)
 MEMBERS = float(FRAMES * TILES * 2 * COLS * (C // GROUPS))
 
 
@@ -41,6 +44,17 @@
     tail = C - 2 * LANES
     rest = jnp.concatenate([rest[:, :tail], rest[:, tail:]], axis=0)
     return jnp.concatenate([packed[:n], packed[n : 2 * n], rest], axis=1)
+
+
+def rows_at(starts, k):
+    return pl.ds(starts[k] * 5 // 2, (starts[k + 1] - starts[k]) * 5 // 2)
+
+
+def joined_dot(pieces, weights):
+    cut = 2 * LANES
+    left = jnp.concatenate([p[:, :cut] for p in pieces] + [p[:, cut:] for p in pieces], axis=1)
+    right = jnp.concatenate([m[:cut] for m in weights] + [m[cut:] for m in weights], axis=0)
+    return jnp.dot(left, right, preferred_element_type=F32)
 
 
 def exact_dot(rows, ones):
@@ -59,10 +73,10 @@
 
 
 def kernel(
-    x_hbm, ws_hbm, wt_hbm, gain1_hbm, shift1_hbm, gain2_hbm, shift2_hbm, bias_hbm, starts_hbm, counts_hbm, out_ref,
-    xv, xf, rows, hrow, hcol, stat, stats, planes, acc, ws, wt, mixed,
-    send_a, send_b, got_a, got_b, passing,
-    gain1, shift1, gain2, shift2, bias, starts, counts, x_sem, w_sem, small_sem, col_ssem, col_rsem, row_ssem, row_rsem, st_ssem, st_rsem, win_ssem, win_rsem, pass_ssem, pass_rsem,
+    x_hbm, ws_hbm, wt_hbm, gain1_hbm, shift1_hbm, gain2_hbm, shift2_hbm, bias_hbm, starts_hbm, counts_hbm, out_hbm,
+    xv, xf, rows, hrow, hcol, stat, stats, planes, acc, ws, wt, merged, out_v,
+    send, got, passing,
+    gain1, shift1, gain2, shift2, bias, starts, counts, x_sem, w_sem, small_sem, out_sem, near_sem, far_sem, col_ssem, col_rsem, row_ssem, row_rsem, st_ssem, st_rsem, win_ssem, win_rsem, pass_ssem, pass_rsem,
 ):
     w = lax.axis_index("win")
     t = lax.axis_index("tile")
@@ -97,20 +111,37 @@
 
     barrier = pltpu.get_barrier_semaphore()
     peers = [(w, (t + i) % TILES) for i in range(1, TILES)]
-    for peer in peers:
-        pl.semaphore_signal(barrier, inc=1, device_id=peer, device_id_type=MESH)
-
     greets = [
         (has_prev, w - 1),
         (has_next, w + 1),
         (relay_up | far_next, w + 2),
         (relay_down | far_prev, w - 2),
     ]
+
+    core, chip = t % 2, t // 2
+    chips = TILES // 2
+    is_near = [jnp.abs(k - chip) <= 2 for k in range(chips)]
+    for k in range(chips):
+
+        @pl.when(chip != k)
+        def _(k=k):
+            at = 2 * k + jnp.where(is_near[k], 1, 0)
+            pl.semaphore_signal(barrier, inc=1, device_id=(w, at), device_id_type=MESH)
+
+    @pl.when(core == 0)
+    def _():
+        pl.semaphore_signal(barrier, inc=1, device_id=(w, t + 1), device_id_type=MESH)
+
     for condition, other in greets:
 
         @pl.when(condition)
         def _(other=other):
-            pl.semaphore_signal(barrier, inc=1, device_id=(other, t), device_id_type=MESH)
+            pl.semaphore_signal(barrier, inc=1, device_id=(other, t - core), device_id_type=MESH)
+
+    near_count = 2 * sum(jnp.where(near, 1, 0) for near in is_near) - 1
+    far_count = 2 * sum(jnp.where(near, 0, 1) for near in is_near) + 2 * sum(
+        jnp.where(condition, 1, 0) for condition, _ in greets
+    )
 
     per = C // GROUPS
     group_of = lax.broadcasted_iota(jnp.int32, (C, 128), 0) // per
@@ -128,14 +159,20 @@
     for y in range(2):
         plane = split[y]
         xf[y] = plane
-        rows[y] = pack(plane).astype(BF16)
+        for k in range(len(ROW_CHUNKS)):
+            part = plane[ROW_STARTS[k] : ROW_STARTS[k + 1]]
+            rows[y, rows_at(ROW_STARTS, k)] = pack(part).astype(BF16)
         total = total + jnp.sum(plane, axis=0, keepdims=True)
         square = square + jnp.sum(plane * plane, axis=0, keepdims=True)
-    stat[0] = exact_dot(jnp.concatenate([total, square], axis=0), to_groups)
-
-    pl.semaphore_wait(
-        barrier, TILES - 1 + sum(jnp.where(condition, 1, 0) for condition, _ in greets)
-    )
+
+    @pl.when(core == 1)
+    def _():
+        pl.semaphore_wait(barrier, near_count)
+        pl.semaphore_signal(near_sem, inc=1, device_id=(w, t - 1), device_id_type=MESH)
+
+    @pl.when(core == 0)
+    def _():
+        pl.semaphore_wait(near_sem, 1)
 
     def remote(src, dst, ssem, rsem, device):
         return pltpu.make_async_remote_copy(
@@ -148,10 +185,6 @@
             remote(stat.at[which], stats.at[which, i], st_ssem.at[which, i], st_rsem.at[which, i], peers[i])
             for i in range(TILES - 1)
         ]
-
-    first_stats = stat_copies(0)
-    for copy in first_stats:
-        copy.start()
 
     lefts, rights = xv.at[0], xv.at[COLS - 1]
     col_plan = [
@@ -168,8 +201,14 @@
     ]
     row_plan = [(down, 1, TCOLS, up), (up, 0, -TCOLS, down)]
     row_copies = [
-        remote(rows.at[y], hrow.at[i], row_ssem.at[i], row_rsem.at[i], (w, (t + by + TILES) % TILES))
-        for i, (_, y, by, _) in enumerate(row_plan)
+        [
+            remote(
+                rows.at[y, rows_at(ROW_STARTS, k)], hrow.at[i, rows_at(ROW_STARTS, k)],
+                row_ssem.at[i, k], row_rsem.at[i, k], (w, (t + by + TILES) % TILES),
+            )
+            for i, (_, y, by, _) in enumerate(row_plan)
+        ]
+        for k in range(len(ROW_CHUNKS))
     ]
 
     def guarded(condition, *actions):
@@ -178,10 +217,28 @@
             for action in actions:
                 action()
 
-    for (sends, _, _, _), copy in zip(col_plan, col_copies):
-        guarded(sends, copy.start)
-    for (sends, _, _, _), copy in zip(row_plan, row_copies):
-        guarded(sends, copy.start)
+    for i in range(2):
+        guarded(row_plan[i][0], row_copies[0][i].start)
+
+    stat[0] = exact_dot(jnp.concatenate([total, square], axis=0), to_groups)
+
+    @pl.when(core == 0)
+    def _():
+        pl.semaphore_wait(barrier, far_count)
+        pl.semaphore_signal(far_sem, inc=1, device_id=(w, t + 1), device_id_type=MESH)
+
+    @pl.when(core == 1)
+    def _():
+        pl.semaphore_wait(far_sem, 1)
+
+    first_stats = stat_copies(0)
+    for copy in first_stats:
+        copy.start()
+    for i in range(6):
+        guarded(col_plan[i][0], col_copies[i].start)
+    for k in range(1, len(ROW_CHUNKS)):
+        for i in range(2):
+            guarded(row_plan[i][0], row_copies[k][i].start)
 
     def finish_stats(which, copies):
         for copy in copies:
@@ -241,13 +298,10 @@
     ws_copy.wait()
 
     def taps(y, rows):
-        summed = None
-        for a in rows:
-            for b in range(3):
-                piece = planes[y + a, FRAMES * b : FRAMES * b + PIX]
-                product = jnp.dot(piece, ws[a, b], preferred_element_type=F32)
-                summed = product if summed is None else summed + product
-        return summed
+        pairs = [(a, b) for a in rows for b in range(3)]
+        return joined_dot(
+            [planes[y + a, FRAMES * b : FRAMES * b + PIX] for a, b in pairs], [ws[a, b] for a, b in pairs]
+        )
 
     acc[0] = taps(0, (1, 2))
     acc[1] = taps(1, (0, 1))
@@ -257,8 +311,10 @@
 
         @pl.when(row_plan[i][3])
         def _(i=i, plane=plane):
-            row_copies[i].wait_recv()
-            planes[plane, FRAMES : FRAMES + PIX] = act(unpack(hrow[i].astype(F32)))
+            for k in range(len(ROW_CHUNKS)):
+                row_copies[k][i].wait_recv()
+                arrived = unpack(hrow[i, rows_at(ROW_STARTS, k)].astype(F32))
+                planes[plane, FRAMES + ROW_STARTS[k] : FRAMES + ROW_STARTS[k + 1]] = act(arrived)
 
         @pl.when(jnp.logical_not(row_plan[i][3]))
         def _(plane=plane):
@@ -315,100 +371,134 @@
     mean2, inverse2 = finish_stats(1, second_stats)
     scale2 = inverse2 * gain2[...].reshape(1, C)
     offset2 = shift2[...].reshape(1, C)
-    for y in range(2):
-        mixed[y * PIX : (y + 1) * PIX] = silu((acc[y] - mean2) * scale2 + offset2).astype(BF16)
 
     wt_copy.wait()
     frame_at = lax.broadcasted_iota(jnp.int32, (PIX, 1), 0) % FRAMES
     def window(index):
         return (lax.clamp(0, index, WINDOWS - 1), t)
 
-    direct_a = [
-        remote(send_a.at[0], got_a.at[1], win_ssem.at[0, 0], win_rsem.at[0, 0], window(w - 1)),
-        remote(send_a.at[1], got_a.at[0], win_ssem.at[1, 0], win_rsem.at[1, 0], window(w + 1)),
-    ]
-    direct_b = [
-        remote(send_b.at[0], got_b.at[1], win_ssem.at[0, 1], win_rsem.at[0, 1], window(w - 1)),
-        remote(send_b.at[1], got_b.at[0], win_ssem.at[1, 1], win_rsem.at[1, 1], window(w + 1)),
-    ]
-    aside = [
-        remote(send_a.at[0], passing, win_ssem.at[0, 0], pass_rsem.at[0], window(w + 1)),
-        remote(send_a.at[1], passing, win_ssem.at[1, 0], pass_rsem.at[0], window(w - 1)),
-    ]
-    onward = [
-        remote(passing, got_a.at[1], pass_ssem.at[0], win_rsem.at[0, 0], window(w - 2)),
-        remote(passing, got_a.at[0], pass_ssem.at[0], win_rsem.at[1, 0], window(w + 2)),
-    ]
+    direct, aside, onward = [], [], []
+    for k in range(len(CHUNKS)):
+        at = rows_at(STARTS, k)
+        direct.append([
+            remote(send.at[0, at], got.at[1, at], win_ssem.at[0, k], win_rsem.at[0, k], window(w - 1)),
+            remote(send.at[1, at], got.at[0, at], win_ssem.at[1, k], win_rsem.at[1, k], window(w + 1)),
+        ])
+        if k < PASSED:
+            aside.append([
+                remote(send.at[0, at], passing.at[at], win_ssem.at[0, k], pass_rsem.at[k], window(w + 1)),
+                remote(send.at[1, at], passing.at[at], win_ssem.at[1, k], pass_rsem.at[k], window(w - 1)),
+            ])
+            onward.append([
+                remote(passing.at[at], got.at[1, at], pass_ssem.at[k], win_rsem.at[0, k], window(w - 2)),
+                remote(passing.at[at], got.at[0, at], pass_ssem.at[k], win_rsem.at[1, k], window(w + 2)),
+            ])
+
+    def send_chunk(k):
+        if k < PASSED:
+            guarded(has_prev & jnp.logical_not(far_prev), direct[k][0].start)
+            guarded(has_next & jnp.logical_not(far_next), direct[k][1].start)
+            guarded(far_prev, aside[k][0].start)
+            guarded(far_next, aside[k][1].start)
+        else:
+            guarded(has_prev, direct[k][0].start)
+            guarded(has_next, direct[k][1].start)
 
     @pl.when(first)
     def _():
-        got_a[0] = jnp.zeros_like(got_a[0])
-        got_b[0] = jnp.zeros_like(got_b[0])
+        got[0] = jnp.zeros_like(got[0])
 
     @pl.when(last)
     def _():
-        got_a[1] = jnp.zeros_like(got_a[1])
-        got_b[1] = jnp.zeros_like(got_b[1])
+        got[1] = jnp.zeros_like(got[1])
 
     frame_rows = COLS * SHARED
-    left_over = []
+    left_over, done = None, 0
     for y in range(2):
-        piece = mixed[y * PIX : (y + 1) * PIX]
-        running = xf[y] + bias[...].reshape(1, C) + jnp.dot(piece, wt[1], preferred_element_type=F32)
-        before = jnp.dot(piece, wt[0], preferred_element_type=F32)
-        running = running + jnp.where(frame_at > 0, pltpu.roll(before, 1, 0), 0.0)
-        after = jnp.dot(piece, wt[2], preferred_element_type=F32)
-        running = running + jnp.where(frame_at < FRAMES - 1, pltpu.roll(after, PIX - 1, 0), 0.0)
+        mixed = silu((acc[y] - mean2) * scale2 + offset2)
+        before = jnp.where(frame_at > 0, pltpu.roll(mixed, 1, 0), 0.0)
+        after = jnp.where(frame_at < FRAMES - 1, pltpu.roll(mixed, PIX - 1, 0), 0.0)
+        running = xf[y] + bias[...].reshape(1, C) + joined_dot(
+            [before.astype(BF16), mixed.astype(BF16), after.astype(BF16)], [wt[k] for k in range(3)]
+        )
         block = running.astype(BF16).astype(F32)
         acc[y] = block
         halves = block.reshape(COLS, 2, SHARED, C)
-        for part in range(2):
-            dense = halves[:, part].reshape(frame_rows, C)
-            if y == 0:
-                send_a[part] = pack(dense[:FIRST]).astype(BF16)
-                left_over.append(dense[FIRST:])
-            else:
-                send_b[part] = pack(jnp.concatenate([left_over[part], dense], axis=0)).astype(BF16)
-        if y == 0:
-            guarded(has_prev & jnp.logical_not(far_prev), direct_a[0].start)
-            guarded(has_next & jnp.logical_not(far_next), direct_a[1].start)
-            guarded(far_prev, aside[0].start)
-            guarded(far_next, aside[1].start)
-    guarded(has_prev, direct_b[0].start)
-    guarded(has_next, direct_b[1].start)
-    guarded(relay_down, aside[0].wait_recv, onward[0].start)
-    guarded(relay_up, aside[1].wait_recv, onward[1].start)
+        dense = [halves[:, part].reshape(frame_rows, C) for part in range(2)]
+        if left_over is not None:
+            dense = [jnp.concatenate([left_over[part], dense[part]], axis=0) for part in range(2)]
+        base = 0 if y == 0 else STARTS[done]
+        for k in range(done, len(CHUNKS)):
+            if STARTS[k + 1] > frame_rows * (y + 1):
+                break
+            for part in range(2):
+                chunk = dense[part][STARTS[k] - base : STARTS[k + 1] - base]
+                send[part, rows_at(STARTS, k)] = pack(chunk).astype(BF16)
+            send_chunk(k)
+            done = k + 1
+        if STARTS[done] < frame_rows * (y + 1):
+            left_over = [dense[part][STARTS[done] - base :] for part in range(2)]
+        else:
+            left_over = None
+    for k in range(PASSED):
+        guarded(relay_down, aside[k][0].wait_recv, onward[k][0].start)
+        guarded(relay_up, aside[k][1].wait_recv, onward[k][1].start)
 
     for (sends, _, _, _), copy in zip(col_plan, col_copies):
         guarded(sends, copy.wait_send)
-    for (sends, _, _, _), copy in zip(row_plan, row_copies):
-        guarded(sends, copy.wait_send)
-    guarded(has_prev, direct_a[1].wait_recv, direct_b[1].wait_recv)
-    guarded(has_next, direct_a[0].wait_recv, direct_b[0].wait_recv)
-    guarded(has_prev, direct_a[0].wait_send, direct_b[0].wait_send)
-    guarded(has_next, direct_a[1].wait_send, direct_b[1].wait_send)
-    guarded(relay_down, onward[0].wait_send)
-    guarded(relay_up, onward[1].wait_send)
+    for k in range(len(ROW_CHUNKS)):
+        for i in range(2):
+            guarded(row_plan[i][0], row_copies[k][i].wait_send)
+    for k in range(len(CHUNKS)):
+        guarded(has_prev, direct[k][1].wait_recv, direct[k][0].wait_send)
+        guarded(has_next, direct[k][0].wait_recv, direct[k][1].wait_send)
+    for k in range(PASSED):
+        guarded(relay_down, onward[k][0].wait_send)
+        guarded(relay_up, onward[k][1].wait_send)
 
     share = 1.0 / denominator
     depth = side * SHARED
 
     def whole(part):
-        return jnp.concatenate([unpack(got_a[part]), unpack(got_b[part])], axis=0)
+        return jnp.concatenate([unpack(got[part, rows_at(STARTS, k)]) for k in range(len(CHUNKS))], axis=0)
 
     prev_all, next_all = whole(0), whole(1)
     own_all = acc[...].reshape(2 * PIX, C)
-    joined = []
+    height = side * FRAMES
+    out_copies = [
+        pltpu.make_async_copy(out_v.at[c], out_hbm.at[:, c], out_sem.at[c]) for c in range(COLS)
+    ]
+    written = 0
     for k in range(5):
         others = jnp.concatenate(
             [prev_all[k * depth : (k + 1) * depth], next_all[k * depth : (k + 1) * depth]], axis=0
         )
         numerator = jnp.dot(blend_matrix, others, preferred_element_type=F32)
-        numerator = numerator + own * own_all[k * side * FRAMES : (k + 1) * side * FRAMES]
-        joined.append(numerator * share)
-    result = jnp.concatenate(joined, axis=0).reshape(2, PIX, C)
-    both = jnp.stack([result[0], result[1]], axis=1).astype(BF16)
-    out_ref[...] = both.reshape(COLS, FRAMES, 2, C)
+        numerator = numerator + own * own_all[k * height : (k + 1) * height]
+        result = numerator * share
+        for y in range(2):
+            low = max(k * height, y * PIX)
+            high = min((k + 1) * height, (y + 1) * PIX)
+            if low >= high:
+                continue
+            part = result[low - k * height : high - k * height]
+            at = pl.ds(2 * (low - y * PIX) + y, high - low, stride=2)
+            for n in range(2):
+                merged[n, at, :] = part[:, n * LANES : (n + 1) * LANES]
+            merged[2, at, : C - 2 * LANES] = part[:, 2 * LANES :]
+        ready = max(0, (k + 1) * side - COLS)
+        if ready > written:
+            for n in range(3):
+                wide = min(LANES, C - n * LANES)
+                piece = merged[n, 2 * FRAMES * written : 2 * FRAMES * ready, :wide].astype(BF16)
+                out_v[written:ready, :, :, n * LANES : n * LANES + wide] = piece.reshape(
+                    ready - written, FRAMES, 2, wide
+                )
+            for c in range(written, ready):
+                out_copies[c].start()
+            written = ready
+    for copy in out_copies:
+        copy.wait()
 
 
 def on_device(
@@ -416,14 +506,13 @@
     temporal_bias, starts, blend_counts,
 ):
     x = jnp.transpose(latents.reshape(FRAMES, 2, COLS, C), (0, 2, 1, 3))
-    vmem = pl.BlockSpec(memory_space=pltpu.VMEM)
     hbm = pl.BlockSpec(memory_space=pltpu.HBM)
     dma = pltpu.SemaphoreType.DMA
     out = pl.pallas_call(
         kernel,
-        out_shape=jax.ShapeDtypeStruct((COLS, FRAMES, 2, C), BF16),
+        out_shape=jax.ShapeDtypeStruct((FRAMES, COLS, 2, C), BF16),
         in_specs=[hbm] * 10,
-        out_specs=vmem,
+        out_specs=hbm,
         scratch_shapes=[
             pltpu.VMEM((COLS, FRAMES, 2, C), BF16),
             pltpu.VMEM((2, PIX, C), F32),
@@ -436,12 +525,11 @@
             pltpu.VMEM((2, PIX, C), F32),
             pltpu.VMEM((3, 3, C, C), BF16),
             pltpu.VMEM((3, C, C), BF16),
-            pltpu.VMEM((2 * PIX, C), BF16),
-            pltpu.VMEM((2, FIRST * 5 // 2, LANES), BF16),
-            pltpu.VMEM((2, SECOND * 5 // 2, LANES), BF16),
-            pltpu.VMEM((2, FIRST * 5 // 2, LANES), BF16),
-            pltpu.VMEM((2, SECOND * 5 // 2, LANES), BF16),
-            pltpu.VMEM((FIRST * 5 // 2, LANES), BF16),
+            pltpu.VMEM((3, 2 * PIX, LANES), F32),
+            pltpu.VMEM((COLS, FRAMES, 2, C), BF16),
+            pltpu.VMEM((2, PACKED, LANES), BF16),
+            pltpu.VMEM((2, PACKED, LANES), BF16),
+            pltpu.VMEM((STARTS[PASSED] * 5 // 2, LANES), BF16),
             pltpu.VMEM((C,), F32),
             pltpu.VMEM((C,), F32),
             pltpu.VMEM((C,), F32),
@@ -452,16 +540,19 @@
             dma((COLS,)),
             dma((2,)),
             dma((7,)),
+            dma((COLS,)),
+            pltpu.SemaphoreType.REGULAR,
+            pltpu.SemaphoreType.REGULAR,
             dma((6,)),
             dma((6,)),
-            dma((2,)),
-            dma((2,)),
+            dma((2, len(ROW_CHUNKS))),
+            dma((2, len(ROW_CHUNKS))),
             dma((2, TILES - 1)),
             dma((2, TILES - 1)),
-            dma((2, 2)),
-            dma((2, 2)),
-            dma((1,)),
-            dma((1,)),
+            dma((2, len(CHUNKS))),
+            dma((2, len(CHUNKS))),
+            dma((PASSED,)),
+            dma((PASSED,)),
         ],
         compiler_params=pltpu.CompilerParams(
             collective_id=0, has_side_effects=True, vmem_limit_bytes=60 << 20
@@ -472,7 +563,7 @@
         x, spatial_weight, temporal_weight, gain_first, shift_first, gain_second, shift_second,
         temporal_bias, starts, blend_counts.T,
     )
-    return jnp.transpose(out, (1, 2, 0, 3)).reshape(1, FRAMES, 1, 2, COLS, C)
+    return jnp.transpose(out, (0, 2, 1, 3)).reshape(1, FRAMES, 1, 2, COLS, C)
 
 
 def solution(mesh):

time: 60 us -> 57.7 us (0.962)
  Pallas kernels: 57.7 us -> 55.3 us
    pallas_call x1, Pallas kernels: 57.7 us -> 55.3 us  [on_device(): pl.pallas_call(kernel, out_shape=jax.ShapeDtypeStruct((FRAMES, COLS, 2, C...]
    reshape x1 -> x0, local copies, waits for them, and re-layouts: 2.15 us -> none  [on_device(): return jnp.transpose(out, (1, 2, 0, 3)).reshape(1, FRAMES, 1, 2, COLS, C)]
    unnamed x0 -> x1, local copies, waits for them, and re-layouts: none -> 2.15 us
where the time goes in v3:
time: 57.7 us; the launch traced here: 57.5 us
  Pallas kernels  55.3 us (96%)
  local copies, waits for them, and re-layouts  2.15 us (4%)
    pallas_call x1, Pallas kernels, on_device(): pl.pallas_call(kernel, out_shape=jax.ShapeDtypeStruct((FRAMES, COLS, 2, C...  55.3 us
    unnamed x1, local copies, waits for them, and re-layouts  2.15 us

profile of v3, /device:TPU:56, one launch (start us, length us, event | category | flops | bytes accessed | tf_op | source)
XLA Modules:
  0.0 57.5 jit_solution(7375159725480629021)
XLA Ops:
  0.0 55.3 %resblock.1 = bf16[16,20,2,320]{3,2,1,0:T(2,128)(2,1)} custom-call(bf16[16,20,2,320]{3,2,1,0:T(2,128)(2,1)} %bitcast.10, bf16[3,3,320,320]{3,2,1,0:T(8,128)(2,1)} %ws_hbm.1, bf16[3,320,320]{2,1,0:T(8,128)(2,1)} %wt_hbm.1, f32[320]{0:T(512)} %gain1_hbm.1, f32[320]{0:T(512)} %shift1_hbm.1, f32[320]{0:T(512)} %gain2_hbm.1, f32[320]{0:T(512)} %shift2_hbm.1, ...), custom_call_target="tpu_custom_call" | custom-call | flops 1600000000 | bytes 4000000 | tf_op jit(solution)/shard_map/resblock/pallas_call | solution.py:511
  55.3 2.1 %copy.13 = bf16[1,16,1,2,20,320]{5,3,4,2,1,0:T(2,128)(2,1)} copy(bf16[1,16,1,2,20,320]{5,3,4,2,1,0:T(2,128)(2,1)} %bitcast.9) | data formatting | bytes 819200

commit v4 on v3

--- a/solution.py
+++ b/solution.py
@@ -24,7 +24,7 @@
 WIDE = (COLS + 2) * FRAMES
 PACKED = PIX * 5 // 2
 SIDE = 8
-CHUNKS = (64, 64, 192)
+CHUNKS = (64, 64, 32, 160)
 PASSED = 2
 STARTS = tuple(sum(CHUNKS[:i]) for i in range(len(CHUNKS) + 1))
 ROW_CHUNKS = (64, 256)
@@ -74,7 +74,7 @@
 
 def kernel(
     x_hbm, ws_hbm, wt_hbm, gain1_hbm, shift1_hbm, gain2_hbm, shift2_hbm, bias_hbm, starts_hbm, counts_hbm, out_hbm,
-    xv, xf, rows, hrow, hcol, stat, stats, planes, acc, ws, wt, merged, out_v,
+    xv, xf, rows, hrow, hcol, stat, stats, planes, acc, ws, wt, out_v,
     send, got, passing,
     gain1, shift1, gain2, shift2, bias, starts, counts, x_sem, w_sem, small_sem, out_sem, near_sem, far_sem, col_ssem, col_rsem, row_ssem, row_rsem, st_ssem, st_rsem, win_ssem, win_rsem, pass_ssem, pass_rsem,
 ):
@@ -466,9 +466,11 @@
     own_all = acc[...].reshape(2 * PIX, C)
     height = side * FRAMES
     out_copies = [
-        pltpu.make_async_copy(out_v.at[c], out_hbm.at[:, c], out_sem.at[c]) for c in range(COLS)
-    ]
-    written = 0
+        pltpu.make_async_copy(
+            out_v.at[pl.ds(k * height, height)], out_hbm.at[pl.ds(k * height, height)], out_sem.at[k]
+        )
+        for k in range(5)
+    ]
     for k in range(5):
         others = jnp.concatenate(
             [prev_all[k * depth : (k + 1) * depth], next_all[k * depth : (k + 1) * depth]], axis=0
@@ -476,27 +478,8 @@
         numerator = jnp.dot(blend_matrix, others, preferred_element_type=F32)
         numerator = numerator + own * own_all[k * height : (k + 1) * height]
         result = numerator * share
-        for y in range(2):
-            low = max(k * height, y * PIX)
-            high = min((k + 1) * height, (y + 1) * PIX)
-            if low >= high:
-                continue
-            part = result[low - k * height : high - k * height]
-            at = pl.ds(2 * (low - y * PIX) + y, high - low, stride=2)
-            for n in range(2):
-                merged[n, at, :] = part[:, n * LANES : (n + 1) * LANES]
-            merged[2, at, : C - 2 * LANES] = part[:, 2 * LANES :]
-        ready = max(0, (k + 1) * side - COLS)
-        if ready > written:
-            for n in range(3):
-                wide = min(LANES, C - n * LANES)
-                piece = merged[n, 2 * FRAMES * written : 2 * FRAMES * ready, :wide].astype(BF16)
-                out_v[written:ready, :, :, n * LANES : n * LANES + wide] = piece.reshape(
-                    ready - written, FRAMES, 2, wide
-                )
-            for c in range(written, ready):
-                out_copies[c].start()
-            written = ready
+        out_v[k * height : (k + 1) * height] = result.astype(BF16)
+        out_copies[k].start()
     for copy in out_copies:
         copy.wait()
 
@@ -510,7 +493,7 @@
     dma = pltpu.SemaphoreType.DMA
     out = pl.pallas_call(
         kernel,
-        out_shape=jax.ShapeDtypeStruct((FRAMES, COLS, 2, C), BF16),
+        out_shape=jax.ShapeDtypeStruct((2 * PIX, C), BF16),
         in_specs=[hbm] * 10,
         out_specs=hbm,
         scratch_shapes=[
@@ -525,8 +508,7 @@
             pltpu.VMEM((2, PIX, C), F32),
             pltpu.VMEM((3, 3, C, C), BF16),
             pltpu.VMEM((3, C, C), BF16),
-            pltpu.VMEM((3, 2 * PIX, LANES), F32),
-            pltpu.VMEM((COLS, FRAMES, 2, C), BF16),
+            pltpu.VMEM((2 * PIX, C), BF16),
             pltpu.VMEM((2, PACKED, LANES), BF16),
             pltpu.VMEM((2, PACKED, LANES), BF16),
             pltpu.VMEM((STARTS[PASSED] * 5 // 2, LANES), BF16),
@@ -563,7 +545,7 @@
         x, spatial_weight, temporal_weight, gain_first, shift_first, gain_second, shift_second,
         temporal_bias, starts, blend_counts.T,
     )
-    return jnp.transpose(out, (0, 2, 1, 3)).reshape(1, FRAMES, 1, 2, COLS, C)
+    return jnp.transpose(out.reshape(2, COLS, FRAMES, C), (2, 0, 1, 3)).reshape(1, FRAMES, 1, 2, COLS, C)
 
 
 def solution(mesh):

time: 57.7 us -> 56.9 us (0.986)
  Pallas kernels: 55.3 us -> 54.4 us
    reshape x0 -> x1, local copies, waits for them, and re-layouts: none -> 2.31 us  [on_device(): out.reshape(2, COLS, FRAMES, C)]
    unnamed x1 -> x0, local copies, waits for them, and re-layouts: 2.15 us -> none
    pallas_call x1, Pallas kernels: 55.3 us -> 54.4 us  [on_device(): pl.pallas_call(kernel, out_shape=jax.ShapeDtypeStruct((2 * PIX, C), BF16)...]
where the time goes in v4:
time: 56.9 us; the launch traced here: 56.7 us
  Pallas kernels  54.4 us (96%)
  local copies, waits for them, and re-layouts  2.31 us (4%)
    pallas_call x1, Pallas kernels, on_device(): pl.pallas_call(kernel, out_shape=jax.ShapeDtypeStruct((2 * PIX, C), BF16)...  54.4 us
    reshape x1, local copies, waits for them, and re-layouts, on_device(): out.reshape(2, COLS, FRAMES, C)  2.31 us

profile of v4, /device:TPU:56, one launch (start us, length us, event | category | flops | bytes accessed | tf_op | source)
XLA Modules:
  0.0 56.7 jit_solution(16411125999849565144)
XLA Ops:
  0.0 54.4 %resblock.1 = bf16[640,320]{1,0:T(8,128)(2,1)} custom-call(bf16[16,20,2,320]{3,2,1,0:T(2,128)(2,1)} %bitcast.11, bf16[3,3,320,320]{3,2,1,0:T(8,128)(2,1)} %ws_hbm.1, bf16[3,320,320]{2,1,0:T(8,128)(2,1)} %wt_hbm.1, f32[320]{0:T(512)} %gain1_hbm.1, f32[320]{0:T(512)} %shift1_hbm.1, f32[320]{0:T(512)} %gain2_hbm.1, f32[320]{0:T(512)} %shift2_hbm.1, ...), custom_call_target="tpu_custom_call" | custom-call | flops 1600000000 | bytes 4000000 | tf_op jit(solution)/shard_map/resblock/pallas_call | solution.py:494
  54.4 2.3 %copy.13 = bf16[2,20,16,320]{3,0,1,2:T(2,128)(2,1)} copy(bf16[2,20,16,320]{3,2,1,0:T(8,128)(2,1)} %bitcast.10) | data formatting | bytes 819200 | tf_op jit(solution)/shard_map/reshape | solution.py:548

commit v5 on v4

--- a/solution.py
+++ b/solution.py
@@ -394,15 +394,21 @@
                 remote(passing.at[at], got.at[0, at], pass_ssem.at[k], win_rsem.at[1, k], window(w + 2)),
             ])
 
+    far = far_prev | far_next
+
     def send_chunk(k):
         if k < PASSED:
-            guarded(has_prev & jnp.logical_not(far_prev), direct[k][0].start)
-            guarded(has_next & jnp.logical_not(far_next), direct[k][1].start)
             guarded(far_prev, aside[k][0].start)
             guarded(far_next, aside[k][1].start)
+            guarded(has_prev & jnp.logical_not(far), direct[k][0].start)
+            guarded(has_next & jnp.logical_not(far), direct[k][1].start)
         else:
-            guarded(has_prev, direct[k][0].start)
-            guarded(has_next, direct[k][1].start)
+            guarded(has_prev & jnp.logical_not(far_next), direct[k][0].start)
+            guarded(has_next & jnp.logical_not(far_prev), direct[k][1].start)
+
+    def send_beside(k):
+        guarded(far_next, direct[k][0].start)
+        guarded(far_prev, direct[k][1].start)
 
     @pl.when(first)
     def _():
@@ -440,6 +446,8 @@
             left_over = [dense[part][STARTS[done] - base :] for part in range(2)]
         else:
             left_over = None
+    for k in range(len(CHUNKS)):
+        send_beside(k)
     for k in range(PASSED):
         guarded(relay_down, aside[k][0].wait_recv, onward[k][0].start)
         guarded(relay_up, aside[k][1].wait_recv, onward[k][1].start)
@@ -449,22 +457,12 @@
     for k in range(len(ROW_CHUNKS)):
         for i in range(2):
             guarded(row_plan[i][0], row_copies[k][i].wait_send)
-    for k in range(len(CHUNKS)):
-        guarded(has_prev, direct[k][1].wait_recv, direct[k][0].wait_send)
-        guarded(has_next, direct[k][0].wait_recv, direct[k][1].wait_send)
-    for k in range(PASSED):
-        guarded(relay_down, onward[k][0].wait_send)
-        guarded(relay_up, onward[k][1].wait_send)
-
     share = 1.0 / denominator
     depth = side * SHARED
 
-    def whole(part):
-        return jnp.concatenate([unpack(got[part, rows_at(STARTS, k)]) for k in range(len(CHUNKS))], axis=0)
-
-    prev_all, next_all = whole(0), whole(1)
     own_all = acc[...].reshape(2 * PIX, C)
     height = side * FRAMES
+    arrived, waited = [[], []], 0
     out_copies = [
         pltpu.make_async_copy(
             out_v.at[pl.ds(k * height, height)], out_hbm.at[pl.ds(k * height, height)], out_sem.at[k]
@@ -472,8 +470,14 @@
         for k in range(5)
     ]
     for k in range(5):
+        while STARTS[waited] < (k + 1) * depth:
+            guarded(has_prev, direct[waited][1].wait_recv)
+            guarded(has_next, direct[waited][0].wait_recv)
+            for part in range(2):
+                arrived[part].append(unpack(got[part, rows_at(STARTS, waited)]))
+            waited += 1
         others = jnp.concatenate(
-            [prev_all[k * depth : (k + 1) * depth], next_all[k * depth : (k + 1) * depth]], axis=0
+            [jnp.concatenate(arrived[part], axis=0)[k * depth : (k + 1) * depth] for part in range(2)], axis=0
         )
         numerator = jnp.dot(blend_matrix, others, preferred_element_type=F32)
         numerator = numerator + own * own_all[k * height : (k + 1) * height]
@@ -482,6 +486,12 @@
         out_copies[k].start()
     for copy in out_copies:
         copy.wait()
+    for k in range(len(CHUNKS)):
+        guarded(has_prev, direct[k][0].wait_send)
+        guarded(has_next, direct[k][1].wait_send)
+    for k in range(PASSED):
+        guarded(relay_down, onward[k][0].wait_send)
+        guarded(relay_up, onward[k][1].wait_send)
 
 
 def on_device(

time: 56.9 us -> 56.6 us (level)
  no operation moved by 1% of the time
where the time goes in v5:
time: 56.6 us; the launch traced here: 56.4 us
  Pallas kernels  54.1 us (96%)
  local copies, waits for them, and re-layouts  2.31 us (4%)
    pallas_call x1, Pallas kernels, on_device(): pl.pallas_call(kernel, out_shape=jax.ShapeDtypeStruct((2 * PIX, C), BF16)...  54.1 us
    reshape x1, local copies, waits for them, and re-layouts, on_device(): out.reshape(2, COLS, FRAMES, C)  2.31 us

profile of v5, /device:TPU:56, one launch (start us, length us, event | category | flops | bytes accessed | tf_op | source)
XLA Modules:
  0.0 56.4 jit_solution(17397164867367790960)
XLA Ops:
  0.0 54.1 %resblock.1 = bf16[640,320]{1,0:T(8,128)(2,1)} custom-call(bf16[16,20,2,320]{3,2,1,0:T(2,128)(2,1)} %bitcast.11, bf16[3,3,320,320]{3,2,1,0:T(8,128)(2,1)} %ws_hbm.1, bf16[3,320,320]{2,1,0:T(8,128)(2,1)} %wt_hbm.1, f32[320]{0:T(512)} %gain1_hbm.1, f32[320]{0:T(512)} %shift1_hbm.1, f32[320]{0:T(512)} %gain2_hbm.1, f32[320]{0:T(512)} %shift2_hbm.1, ...), custom_call_target="tpu_custom_call" | custom-call | flops 1600000000 | bytes 4000000 | tf_op jit(solution)/shard_map/resblock/pallas_call | solution.py:504
  54.1 2.3 %copy.13 = bf16[2,20,16,320]{3,0,1,2:T(2,128)(2,1)} copy(bf16[2,20,16,320]{3,2,1,0:T(8,128)(2,1)} %bitcast.10) | data formatting | bytes 819200 | tf_op jit(solution)/shard_map/reshape | solution.py:558
